TPU v7x, 512 devices: a whole 4x4x16 slice. The times are simulated.
512 devices in a mesh: dp: 16 (over x, y), tensor: 32 (over z, core).
Axes of the slice: x: 4, y: 4, z: 16, core: 2. Of those that a mesh axis runs over, the one named last changes fastest.
Arguments:
- tokens: bfloat16 [2048, 4096], P('dp', 'tensor'), may hold values from -6 to 6
- w_in: bfloat16 [4096, 8192], P('dp', 'tensor'), may hold values from -0.09375 to 0.09375
- conv_weight: float32 [4, 8192], P(None, 'tensor'), may hold values from -3 to 3
- w_dtlow: bfloat16 [8192, 512], P('tensor'), may hold values from -0.0625 to 0.0625
- w_bc: bfloat16 [8192, 32], P('tensor'), may hold values from -0.0625 to 0.0625
- w_dt: bfloat16 [512, 8192], P(None, 'tensor'), may hold values from -0.25 to 0.25
- dt_bias: float32 [8192], P('tensor'), may hold values from -4 to -1
- a_log: float32 [8192, 16], P('tensor'), may hold values from -3 to 0.7
- d_skip: float32 [8192], P('tensor'), may hold values from 0.5 to 2
- w_out: bfloat16 [8192, 4096], P('tensor', 'dp'), may hold values from -0.0625 to 0.0625
- cotangent: bfloat16 [2048, 4096], P('dp', 'tensor'), may hold values from -6 to 6
- err_in: float32 [4096, 8192], P('dp', 'tensor'), may hold values from -1.8 to 1.8
- err_out: float32 [8192, 4096], P('tensor', 'dp'), may hold values from -1.8 to 1.8
Outputs:
- mixed: bfloat16 [2048, 4096], P('dp', 'tensor')
- input_grad: bfloat16 [2048, 4096], P('dp', 'tensor')
- update_in: float32 [4096, 8192], P('dp', 'tensor')
- residue_in: float32 [4096, 8192], P('dp', 'tensor')
- update_out: float32 [8192, 4096], P('tensor', 'dp')
- residue_out: float32 [8192, 4096], P('tensor', 'dp')
All inputs are finite; a program needn't handle non-finite values. Where the computation divides by a largest or mean magnitude, that divisor is 1e-20 or more.
Results may differ from a plain program's by a relative error of at most 0.035.
Values may be sent and summed in bfloat16 or wider, within the bound.
No kernel may reach another device: no remote copies, remote signals or barrier semaphores. Data moves between devices by JAX's collectives and lax.ppermute only.
A program may use at most 128 MiB of HBM per device.

v0:
```python
import jax
import jax.numpy as jnp
from jax import lax
from jax.experimental import pallas as pl
from jax.experimental.pallas import tpu as pltpu
from jax.sharding import PartitionSpec as P

QB = 128


eps_scale = 1e-06


def contract(left, right, left_dim, right_dim):
    return lax.dot_general(
        left, right, (((left_dim,), (right_dim,)), ((), ())), preferred_element_type=jnp.float32
    )


def identity(size):
    rows = lax.broadcasted_iota(jnp.int32, (size, size), 0)
    cols = lax.broadcasted_iota(jnp.int32, (size, size), 1)
    return jnp.where(rows == cols, 1.0, 0.0).astype(jnp.bfloat16)


def scan_kernel(
    small_ref, w_dt_ref, bias_ref, a_neg_ref, skip_ref, conv_ref, dh_ref,
    hidden_ref, dconv_ref, back_ref,
    delta_s, x_s, u_s, y_s, dd_s, states,
):
    tokens, channels = conv_ref.shape
    n = a_neg_ref.shape[0]
    rank = w_dt_ref.shape[0]
    low = small_ref[:, :rank]
    pre = jnp.dot(low, w_dt_ref[...], preferred_element_type=jnp.float32) + bias_ref[...]
    delta = jax.nn.softplus(pre)
    x = conv_ref[...].astype(jnp.float32)
    delta_s[...] = delta
    x_s[...] = x
    u_s[...] = delta * x
    maps = contract(identity(2 * n), small_ref[:, rank:], 1, 1)
    a_neg = a_neg_ref[...]
    skip = skip_ref[...]
    states[0] = jnp.zeros((n, channels), jnp.float32)

    def columns(rolled, row, j):
        return jnp.broadcast_to(rolled[row : row + n, j : j + 1], (n, channels))

    def forward(chunk, h):
        start = pl.multiple_of(chunk * 8, 8)
        d8 = delta_s[pl.ds(start, 8), :]
        x8 = x_s[pl.ds(start, 8), :]
        u8 = u_s[pl.ds(start, 8), :]
        rolled = pltpu.roll(maps, lax.rem(tokens - start, tokens), 1)
        rows = []
        for j in range(8):
            h = jnp.exp(d8[j : j + 1] * a_neg) * h + u8[j : j + 1] * columns(rolled, 0, j)
            states[start + j + 1] = h
            rows.append(jnp.sum(h * columns(rolled, n, j), axis=0, keepdims=True))
        y_s[pl.ds(start, 8), :] = jnp.concatenate(rows, axis=0) + skip * x8
        return h

    lax.fori_loop(0, tokens // 8, forward, jnp.zeros((n, channels), jnp.float32))
    hidden_ref[...] = y_s[...].astype(hidden_ref.dtype)
    lane = lax.broadcasted_iota(jnp.int32, (n, tokens), 1)

    def backward(step, carry):
        g_next, acc_b, acc_c = carry
        start = pl.multiple_of(tokens - 8 - step * 8, 8)
        d8 = delta_s[pl.ds(start, 8), :]
        x8 = x_s[pl.ds(start, 8), :]
        u8 = u_s[pl.ds(start, 8), :]
        dy8 = dh_ref[pl.ds(start, 8), :]
        rolled = pltpu.roll(maps, lax.rem(tokens - start, tokens), 1)
        rows_a, rows_b = [None] * 8, [None] * 8
        for j in range(7, -1, -1):
            dy = dy8[j : j + 1]
            g = g_next + dy * columns(rolled, n, j)
            here = lane == start + j
            acc_c = jnp.where(here, jnp.sum(dy * states[start + j + 1], axis=1, keepdims=True), acc_c)
            acc_b = jnp.where(here, jnp.sum(g * u8[j : j + 1], axis=1, keepdims=True), acc_b)
            rows_b[j] = jnp.sum(g * columns(rolled, 0, j), axis=0, keepdims=True)
            g_next = g * jnp.exp(d8[j : j + 1] * a_neg)
            rows_a[j] = jnp.sum(g_next * (states[start + j] * a_neg), axis=0, keepdims=True)
        sum_b = jnp.concatenate(rows_b, axis=0)
        dd_s[pl.ds(start, 8), :] = jnp.concatenate(rows_a, axis=0) + x8 * sum_b
        dconv_ref[pl.ds(start, 8), :] = d8 * sum_b + skip * dy8
        return g_next, acc_b, acc_c

    zero = jnp.zeros((n, tokens), jnp.float32)
    _, acc_b, acc_c = lax.fori_loop(
        0, tokens // 8, backward, (jnp.zeros((n, channels), jnp.float32), zero, zero)
    )
    d_pre = (dd_s[...] * jax.nn.sigmoid(pre)).astype(jnp.bfloat16)
    back_ref[:, :rank] = contract(d_pre, w_dt_ref[...], 1, 1).astype(back_ref.dtype)
    both = jnp.concatenate([acc_b, acc_c], axis=0).astype(jnp.bfloat16)
    back_ref[:, rank:] = contract(identity(tokens), both, 1, 1).astype(back_ref.dtype)


VMEM_BYTES = 16 << 20


def local_call(kernel, shapes, scratch=(), specs=None):
    more = {} if specs is None else {"grid": (1,), "in_specs": specs}
    return pl.pallas_call(
        kernel,
        **more,
        out_shape=tuple(jax.ShapeDtypeStruct(shape, kind) for shape, kind in shapes),
        scratch_shapes=list(scratch),
        compiler_params=pltpu.CompilerParams(vmem_limit_bytes=VMEM_BYTES),
    )


def pair_kernel(keep_ref, give_ref, *refs):
    refs[-1][...] = (keep_ref[...].astype(jnp.float32) + give_ref[...].astype(jnp.float32)).astype(jnp.bfloat16)


def pairs_kernel(keep_out_ref, give_out_ref, keep_in_ref, give_in_ref, total_ref):
    rows = keep_out_ref.shape[1]
    out = keep_out_ref[...] + give_out_ref[...].astype(jnp.float32)
    total_ref[:, :rows, :] = out.astype(jnp.bfloat16)
    grad = keep_in_ref[...] + give_in_ref[...].astype(jnp.float32)
    total_ref[:, rows:, :] = grad.astype(jnp.bfloat16)


def share_kernel(parts_ref, *refs):
    total = jnp.sum(parts_ref[...].astype(jnp.float32), axis=0).astype(jnp.bfloat16)
    refs[-1][...] = jnp.broadcast_to(total[None], parts_ref.shape)


def pack_kernel(mine_ref, other_ref, block_ref, packed_ref):
    chips, height, lanes = packed_ref.shape
    rows, width = mine_ref.shape
    ahead = height - rows
    total = mine_ref[...].astype(jnp.float32) + other_ref[...].astype(jnp.float32)
    tiles = pl.cdiv(width, lanes)
    total = jnp.concatenate([total, jnp.zeros((rows, tiles * lanes - width), jnp.float32)], axis=1)
    share = total.reshape(chips, rows // chips, tiles * lanes)
    pieces = [share[:, :, i * lanes : (i + 1) * lanes] for i in range(tiles)]
    spare = ahead - tiles * (rows // chips)
    if spare:
        pieces.append(jnp.zeros((chips, spare, lanes), jnp.float32))
    packed_ref[:, :ahead, :] = jnp.concatenate(pieces, axis=1).astype(jnp.bfloat16)
    packed_ref[:, ahead:, :] = jnp.broadcast_to(block_ref[...][None], (chips, rows, lanes))


def unpack_kernel(parts_ref, after_ref, total_ref):
    _, height, width = total_ref.shape
    lanes = parts_ref.shape[2]
    total = jnp.sum(parts_ref[...].astype(jnp.float32), axis=0)
    pieces = [total[i * height : (i + 1) * height] for i in range(pl.cdiv(width, lanes))]
    total = jnp.concatenate(pieces, axis=1)[:, :width].astype(jnp.bfloat16)
    total_ref[...] = jnp.broadcast_to(total[None], total_ref.shape)


def in_order(even, mine, other):
    return jnp.concatenate([jnp.where(even, mine, other), jnp.where(even, other, mine)], axis=1)


def inner_kernel(
    mine_ref, other_ref, even_ref, w_in_ref, taps_ref, low_ref, bc_ref,
    whole_ref, pre_ref, conv_ref, small_ref, total_s,
):
    chips, rows, block = mine_ref.shape
    even = even_ref[...] > 0

    def step(chip, carry):
        features = in_order(even, mine_ref[chip], other_ref[chip])
        whole_ref[chip] = features
        total_s[...] += jnp.dot(features, w_in_ref[chip], preferred_element_type=jnp.float32)
        return carry

    total_s[...] = jnp.zeros_like(total_s)
    lax.fori_loop(0, chips, step, 0, unroll=4)
    inner = total_s[...].astype(jnp.bfloat16).astype(jnp.float32)
    taps = taps_ref[...]
    width = taps.shape[0]
    row = lax.broadcasted_iota(jnp.int32, inner.shape, 0)
    pre = taps[width - 1 :] * inner
    for back in range(1, width):
        shifted = jnp.where(row >= back, pltpu.roll(inner, back, 0), 0.0)
        pre = pre + taps[width - 1 - back : width - back] * shifted
    conv = (pre / (1.0 + jnp.exp(-pre))).astype(jnp.bfloat16)
    pre_ref[...] = pre
    conv_ref[...] = conv
    rank = low_ref.shape[1]
    small_ref[:, :rank] = jnp.dot(conv, low_ref[...], preferred_element_type=jnp.float32).astype(jnp.bfloat16)
    small_ref[:, rank:] = jnp.dot(conv, bc_ref[...], preferred_element_type=jnp.float32).astype(jnp.bfloat16)


def cotangent_kernel(mine_ref, other_ref, even_ref, w_out_ref, whole_ref, hidden_ref):
    chips = w_out_ref.shape[0]
    even = even_ref[...] > 0

    def step(chip, carry):
        features = in_order(even, mine_ref[chip], other_ref[chip])
        whole_ref[chip] = features
        hidden_ref[...] += contract(features, w_out_ref[chip], 1, 1)
        return carry

    hidden_ref[...] = jnp.zeros_like(hidden_ref)
    lax.fori_loop(0, chips, step, 0, unroll=4)


def coded(part):
    scale = (jnp.max(jnp.abs(part), axis=1, keepdims=True) + eps_scale).astype(jnp.bfloat16)
    scale = scale.astype(jnp.float32)
    return (part / scale).astype(jnp.bfloat16).astype(jnp.float32) * scale


def split_parts(even, part, keep_ref, give_ref, chip):
    first, second = coded(part[:, :QB]), coded(part[:, QB:])
    keep_ref[chip] = jnp.where(even, first, second)
    give_ref[chip] = jnp.where(even, second, first).astype(give_ref.dtype)


def soft_sign(grad):
    signs = []
    for start in range(0, grad.shape[1], QB):
        part = grad[:, start : start + QB]
        mean = jnp.mean(jnp.abs(part), axis=1, keepdims=True) + eps_scale
        signs.append(jnp.tanh(part / mean).astype(jnp.bfloat16))
    return jnp.concatenate(signs, axis=1)


def sign_out_kernel(hidden_ref, cot_ref, after_ref, sign_ref):
    hidden = hidden_ref[...]

    def step(chip, carry):
        sign_ref[chip] = soft_sign(contract(hidden, cot_ref[chip], 0, 0))
        return carry

    lax.fori_loop(0, cot_ref.shape[0], step, 0, unroll=2)


def out_kernel(hidden_ref, w_out_ref, even_ref, after_ref, keep_ref, give_ref):
    hidden = hidden_ref[...]
    even = even_ref[...] > 0

    def step(chip, carry):
        part = jnp.dot(hidden, w_out_ref[chip], preferred_element_type=jnp.float32)
        split_parts(even, part, keep_ref, give_ref, chip)
        return carry

    lax.fori_loop(0, w_out_ref.shape[0], step, 0, unroll=2)


def sign_in_kernel(
    back_ref, low_ref, bc_ref, d_conv_ref, pre_ref, taps_ref, whole_ref, d_inner_ref, sign_ref
):
    rank = low_ref.shape[1]
    back = back_ref[...]
    d_conv = (
        d_conv_ref[...]
        + contract(back[:, :rank], low_ref[...], 1, 1)
        + contract(back[:, rank:], bc_ref[...], 1, 1)
    )
    pre = pre_ref[...]
    gate = jax.nn.sigmoid(pre)
    d_sum = d_conv * (gate * (1.0 + pre * (1.0 - gate)))
    taps = taps_ref[...]
    width = taps.shape[0]
    rows = d_sum.shape[0]
    row = lax.broadcasted_iota(jnp.int32, d_sum.shape, 0)
    d_inner = taps[width - 1 :] * d_sum
    for ahead in range(1, width):
        shifted = jnp.where(row < rows - ahead, pltpu.roll(d_sum, rows - ahead, 0), 0.0)
        d_inner = d_inner + taps[width - 1 - ahead : width - ahead] * shifted
    d_inner = d_inner.astype(jnp.bfloat16)
    d_inner_ref[...] = d_inner

    def step(chip, carry):
        side = sign_ref.shape[0]
        sign_ref[lax.rem(chip, side), lax.div(chip, side)] = soft_sign(contract(whole_ref[chip], d_inner, 0, 0))
        return carry

    lax.fori_loop(0, whole_ref.shape[0], step, 0, unroll=2)


def grad_kernel(d_inner_ref, w_in_ref, even_ref, keep_ref, give_ref):
    d_inner = d_inner_ref[...]
    even = even_ref[...] > 0

    def step(chip, carry):
        part = contract(d_inner, w_in_ref[chip], 1, 1)
        split_parts(even, part, keep_ref, give_ref, chip)
        return carry

    lax.fori_loop(0, w_in_ref.shape[0], step, 0, unroll=2)


def on_device(
    tokens,
    w_in,
    conv_weight,
    w_dtlow,
    w_bc,
    w_dt,
    dt_bias,
    a_log,
    d_skip,
    w_out,
    cotangent,
    err_in,
    err_out,
):
    tensor = lax.axis_size("tensor")
    replicas = lax.axis_size("dp")
    rows, block = tokens.shape
    chips = tensor // 2
    side = int(replicas**0.5)
    channels = w_in.shape[1]
    width = w_in.shape[0]
    rank = w_dt.shape[0]
    small_width = rank + w_bc.shape[1]
    bf16, f32 = jnp.bfloat16, jnp.float32
    ring = [list(range(core, tensor, 2)) for core in range(2)]
    swap = [(i, i ^ 1) for i in range(tensor)]
    core = lax.rem(lax.axis_index("tensor"), 2)
    even = jnp.full((1, 1), 1 - core, jnp.int32)

    def exchange(parts, axis, groups=None):
        return lax.all_to_all(
            parts, axis, split_axis=0, concat_axis=0, tiled=True, axis_index_groups=groups
        )

    def spread(value, axis, size, groups=None):
        return exchange(jnp.broadcast_to(value[None], (size, *value.shape)), axis, groups)

    def other_core(value):
        return lax.ppermute(value, "tensor", swap)

    inside, left = pl.BlockSpec(memory_space=pltpu.VMEM), pl.BlockSpec(memory_space=pl.ANY)

    def pair_sum(keep, give, *after):
        (total,) = local_call(
            pair_kernel, ((keep.shape, bf16),), specs=[inside, inside] + [left] * len(after)
        )(keep, other_core(give), *after)
        return total

    def sum_channels(chip, *after):
        share = exchange(chip.reshape(chips, rows // chips, chip.shape[1]), "tensor", ring)
        (total,) = local_call(
            share_kernel, ((share.shape, bf16),), specs=[inside] + [left] * len(after)
        )(share, *after)
        return exchange(total, "tensor", ring).reshape(chip.shape)

    def to_owner(array, shift_of, stride):
        place = shift_of(lax.axis_index("dp"))

        def entry(ahead):
            return lax.dynamic_index_in_dim(array, lax.rem(place + ahead, side), 0, False)

        total = entry(0).astype(f32)
        for ahead in range(1, side):
            perm = [
                (i, i + ((shift_of(i) + ahead) % side - shift_of(i)) * stride) for i in range(replicas)
            ]
            total = total + lax.ppermute(entry(ahead), "dp", perm).astype(f32)
        return total

    def along_x(parts):
        return to_owner(parts, lambda i: i // side, side)

    def along_y(parts):
        return to_owner(parts, lambda i: i % side, 1)

    w_in_full = spread(w_in, "dp", replicas)
    w_out_full = lax.all_gather(w_out, "dp", axis=0)
    mine = lax.all_gather(tokens, "tensor", axis=0, axis_index_groups=ring)
    whole, pre, conv_out, small = local_call(
        inner_kernel,
        (
            ((chips, rows, 2 * block), bf16),
            ((rows, channels), f32),
            ((rows, channels), bf16),
            ((rows, small_width), bf16),
        ),
        [pltpu.VMEM((rows, channels), f32)],
    )(mine, other_core(mine), even, w_in_full, conv_weight, w_dtlow, w_bc)
    tiles = pl.cdiv(small_width, block)
    ahead = pl.cdiv(tiles * (rows // chips), 16) * 16
    (packed,) = local_call(pack_kernel, (((chips, ahead + rows, block), bf16),))(
        small, other_core(small), cotangent
    )
    packed = exchange(packed, "tensor", ring)
    (total,) = local_call(
        unpack_kernel,
        (((chips, rows // chips, small_width), bf16),),
        specs=[pl.BlockSpec((chips, ahead, block), lambda step: (0, 0, 0)), left],
    )(packed, w_out_full)
    small = exchange(total, "tensor", ring).reshape(rows, small_width)
    cot_mine = packed[:, ahead:]
    cot_whole, d_hidden = local_call(
        cotangent_kernel,
        (((chips, rows, 2 * block), bf16), ((rows, channels), f32)),
    )(cot_mine, other_core(cot_mine), even, w_out_full)
    hidden_out, d_conv, back = local_call(
        scan_kernel,
        (((rows, channels), bf16), ((rows, channels), f32), ((rows, small_width), bf16)),
        [pltpu.VMEM((rows, channels), f32)] * 5
        + [pltpu.VMEM((rows + 1, a_log.shape[1], channels), f32)],
    )(small, w_dt, dt_bias[None, :], -jnp.exp(a_log).T, d_skip[None, :], conv_out, d_hidden)
    back_chip = pair_sum(back, back)
    (sign_out,) = local_call(sign_out_kernel, (((chips, width, channels), bf16),), specs=[inside, inside, left])(
        hidden_out, cot_whole, back_chip
    )
    out_parts = local_call(
        out_kernel,
        (((chips, rows, block), f32), ((chips, rows, block), bf16)),
        specs=[inside] * 3 + [left],
    )(hidden_out, w_out_full, even, back_chip)
    back = sum_channels(back_chip, sign_out, *out_parts)
    d_inner, sign_in = local_call(
        sign_in_kernel,
        (((rows, channels), bf16), ((side, side, width, channels), bf16)),
    )(back, w_dtlow, w_bc, d_conv, pre, conv_weight, whole)
    votes_in = along_x(along_y(sign_in).astype(bf16))
    votes_out = along_y(along_x(sign_out.reshape(side, side, width, channels)).astype(bf16))
    grad_parts = local_call(
        grad_kernel,
        (((chips, rows, block), f32), ((chips, rows, block), bf16)),
    )(d_inner, w_in_full, even)
    (parts,) = local_call(pairs_kernel, (((chips, 2 * rows, block), bf16),))(
        out_parts[0], other_core(out_parts[1]), grad_parts[0], other_core(grad_parts[1])
    )
    sums = jnp.sum(exchange(parts, "tensor", ring).astype(f32), axis=0).astype(bf16)
    merged_in = votes_in / replicas + err_in
    merged_out = votes_out / replicas + err_out
    update_in = jnp.tanh(4.0 * merged_in)
    update_out = jnp.tanh(4.0 * merged_out)
    return (
        sums[:rows],
        sums[rows:],
        update_in,
        merged_in - update_in,
        update_out,
        merged_out - update_out,
    )


def solution(mesh):
    return jax.shard_map(
        on_device,
        mesh=mesh,
        in_specs=(
            P("dp", "tensor"),
            P("dp", "tensor"),
            P(None, "tensor"),
            P("tensor", None),
            P("tensor", None),
            P(None, "tensor"),
            P("tensor"),
            P("tensor", None),
            P("tensor"),
            P("tensor", "dp"),
            P("dp", "tensor"),
            P("dp", "tensor"),
            P("tensor", "dp"),
        ),
        out_specs=(
            P("dp", "tensor"),
            P("dp", "tensor"),
            P("dp", "tensor"),
            P("dp", "tensor"),
            P("tensor", "dp"),
            P("tensor", "dp"),
        ),
        check_vma=False,
    )
```

profile of v0, /device:TPU:1, one launch (start us, length us, event | category | flops | bytes accessed | tf_op | source)
XLA Modules:
  0.0 294.7 jit_solution(12087767464905253977)
XLA Ops:
  9.6 7.7 %all-to-all-start = ((bf16[16,256,256]{2,1,0:T(8,128)(2,1)}), bf16[16,256,256]{2,1,0:T(8,128)(2,1)S(1)}, u32[]{:S(2)}, u32[]{:S(2)}) async-start(bf16[16,256,256]{2,1,0:T(8,128)(2,1)} %broadcast_in_dim.16), calls=%async_computation | async-start | bytes 4194304 | tf_op jit(solution)/shard_map/all_to_all | solution.py:323
  18.1 33.2 %all-gather = bf16[2048,128]{1,0:T(8,128)(2,1)S(1)} all-gather(bf16[128,128]{1,0:T(8,128)(2,1)S(1)} %copy-done.29), channel_id=2, replica_groups={{0,2,4,6,8,10,12,14,16,18,20,22,24,26,28,30},{1,3,5,7,9,11,13,15,17,19,..., dimensions={0}, use_global_device_ids=true | all-gather | bytes 557056 | tf_op jit(solution)/shard_map/all_gather | solution.py:370
  51.3 8.0 %collective-permute-start = (bf16[16,128,128]{2,1,0:T(8,128)(2,1)S(1)}, bf16[16,128,128]{2,1,0:T(8,128)(2,1)S(1)}, u32[]{:S(2)}, u32[]{:S(2)}) collective-permute-start(bf16[16,128,128]{2,1,0:T(8,128)(2,1)S(1)} %bitcast.52), channel_id=1, source_target_pairs={{0,1},{1,0},{2,3},{3,2},{4,5},{5,4},{6,7},{7,6},{8,9},{9,8},{10,11... | collective-permute-start | bytes 1572872 | tf_op jit(solution)/shard_map/ppermute | solution.py:331
  67.4 41.0 %all_to_all.30.parts_ref = bf16[16,176,128]{2,1,0:T(8,128)(2,1)S(1)} all-to-all(bf16[16,176,128]{2,1,0:T(8,128)(2,1)S(1)} %shard_map.173), channel_id=1, replica_groups={{0,2,4,6,8,10,12,14,16,18,20,22,24,26,28,30},{1,3,5,7,9,11,13,15,17,19,..., dimensions={0} | all-to-all | bytes 1441792 | tf_op jit(solution)/shard_map/all_to_all | solution.py:323
  108.4 6.5 %collective-permute-start.2 = (bf16[16,128,128]{2,1,0:T(8,128)(2,1)S(1)}, bf16[16,128,128]{2,1,0:T(8,128)(2,1)}, u32[]{:S(2)}, u32[]{:S(2)}) collective-permute-start(bf16[16,128,128]{2,1,0:T(8,128)(2,1)S(1)} %slice.12.mine_ref), channel_id=1, source_target_pairs={{0,1},{1,0},{2,3},{3,2},{4,5},{5,4},{6,7},{7,6},{8,9},{9,8},{10,11... | collective-permute-start | bytes 1572872 | tf_op jit(solution)/shard_map/ppermute | solution.py:331
  117.2 5.4 %all-to-all-start.2 = ((bf16[16,8,544]{2,1,0:T(8,128)(2,1)}), bf16[16,8,544]{2,1,0:T(8,128)(2,1)S(1)}, u32[]{:S(2)}, u32[]{:S(2)}) async-start(bf16[16,8,544]{2,1,0:T(8,128)(2,1)} %shard_map.174), calls=%async_computation.2 | async-start | bytes 327680 | tf_op jit(solution)/shard_map/all_to_all | solution.py:323
  126.7 8.8 %all-to-all-done.2 = bf16[16,8,544]{2,1,0:T(8,128)(2,1)S(1)} async-done(((bf16[16,8,544]{2,1,0:T(8,128)(2,1)}), bf16[16,8,544]{2,1,0:T(8,128)(2,1)S(1)}, u32[]{:S(2)}, u32[]{:S(2)}) %all-to-all-start.2) | async-done | bytes 139296 | tf_op jit(solution)/shard_map/all_to_all | solution.py:323
  136.4 11.0 %shard_map.176 = (bf16[128,256]{1,0:T(8,128)(2,1)S(1)}, f32[128,256]{1,0:T(8,128)S(1)}, bf16[128,544]{1,0:T(8,128)(2,1)S(1)}) custom-call(bf16[128,544]{1,0:T(8,128)(2,1)S(1)} %bitcast.54, bf16[512,256]{1,0:T(8,128)(2,1)S(1)} %copy-done.16, f32[1,256]{1,0:T(1,128)S(1)} %bitcast.55, f32[16,256]{1,0:T(8,128)S(1)} %negate_bitcast_fusion.a_neg_ref, ...), custom_call_target="tpu_custom_call" | custom-call | tf_op jit(solution)/shard_map/pallas_call | solution.py:398
  147.4 4.0 %collective-permute-start.3 = (bf16[128,544]{1,0:T(8,128)(2,1)S(1)}, bf16[128,544]{1,0:T(8,128)(2,1)S(1)}, u32[]{:S(2)}, u32[]{:S(2)}) collective-permute-start(bf16[128,544]{1,0:T(8,128)(2,1)S(1)} %get-tuple-element.25.keep_ref), channel_id=1, source_target_pairs={{0,1},{1,0},{2,3},{3,2},{4,5},{5,4},{6,7},{7,6},{8,9},{9,8},{10,11... | collective-permute-start | bytes 417800 | tf_op jit(solution)/shard_map/ppermute | solution.py:331
  153.2 5.6 %all-to-all-start.3 = ((bf16[16,8,544]{2,1,0:T(8,128)(2,1)}), bf16[16,8,544]{2,1,0:T(8,128)(2,1)S(1)}, u32[]{:S(2)}, u32[]{:S(2)}) async-start(bf16[16,8,544]{2,1,0:T(8,128)(2,1)} %bitcast.7), calls=%async_computation.3 | async-start | bytes 327680 | tf_op jit(solution)/shard_map/all_to_all | solution.py:323
  162.3 3.3 %shard_map.179.refs_0_ = bf16[16,256,256]{2,1,0:T(8,128)(2,1)S(1)} custom-call(bf16[128,256]{1,0:T(8,128)(2,1)S(1)} %get-tuple-element.24.hidden_ref, bf16[16,128,256]{2,1,0:T(8,128)(2,1)S(1)} %copy-done.6, bf16[128,544]{1,0:T(8,128)(2,1)} %shard_map.177.after_ref), custom_call_target="tpu_custom_call" | custom-call | tf_op jit(solution)/shard_map/pallas_call | solution.py:405
  165.7 5.5 %all-to-all-done.3.parts_ref = bf16[16,8,544]{2,1,0:T(8,128)(2,1)S(1)} async-done(((bf16[16,8,544]{2,1,0:T(8,128)(2,1)}), bf16[16,8,544]{2,1,0:T(8,128)(2,1)S(1)}, u32[]{:S(2)}, u32[]{:S(2)}) %all-to-all-start.3) | async-done | bytes 139296 | tf_op jit(solution)/shard_map/all_to_all | solution.py:323
  174.5 7.7 %all-to-all-start.4 = ((bf16[16,8,544]{2,1,0:T(8,128)(2,1)}), bf16[16,8,544]{2,1,0:T(8,128)(2,1)}, u32[]{:S(2)}, u32[]{:S(2)}) async-start(bf16[16,8,544]{2,1,0:T(8,128)(2,1)} %copy-done.13), calls=%async_computation.4 | async-start | bytes 327680 | tf_op jit(solution)/shard_map/all_to_all | solution.py:323
  185.0 9.5 %all-to-all-done.4 = bf16[16,8,544]{2,1,0:T(8,128)(2,1)} async-done(((bf16[16,8,544]{2,1,0:T(8,128)(2,1)}), bf16[16,8,544]{2,1,0:T(8,128)(2,1)}, u32[]{:S(2)}, u32[]{:S(2)}) %all-to-all-start.4) | async-done | bytes 139296 | tf_op jit(solution)/shard_map/all_to_all | solution.py:323
  197.5 4.6 %shard_map.181 = (bf16[128,256]{1,0:T(8,128)(2,1)S(1)}, bf16[4,4,256,256]{3,2,1,0:T(8,128)(2,1)S(1)}) custom-call(bf16[128,544]{1,0:T(8,128)(2,1)} %bitcast.8.back_ref, bf16[256,512]{1,0:T(8,128)(2,1)S(1)} %copy-done.8, bf16[256,32]{1,0:T(8,128)(2,1)S(1)} %copy.19.bc_ref, f32[128,256]{1,0:T(8,128)S(1)} %copy-done.20, f32[128,256]{1,0:T(8,128)S(1)} %copy-done.18, ...), custom_call_target="tpu_custom_call" | custom-call | tf_op jit(solution)/shard_map/pallas_call | solution.py:414
  205.0 3.0 %shard_map.182 = (f32[16,128,128]{2,1,0:T(8,128)S(1)}, bf16[16,128,128]{2,1,0:T(8,128)(2,1)S(1)}) custom-call(bf16[128,256]{1,0:T(8,128)(2,1)S(1)} %get-tuple-element.32.d_inner_ref, bf16[16,256,256]{2,1,0:T(8,128)(2,1)S(1)} %copy-done.1, s32[1,1]{1,0:T(1,128)} %bitcast.1.even_ref), custom_call_target="tpu_custom_call" | custom-call | tf_op jit(solution)/shard_map/pallas_call | solution.py:420
  208.0 6.2 %collective-permute-start.5 = (bf16[16,128,128]{2,1,0:T(8,128)(2,1)S(1)}, bf16[16,128,128]{2,1,0:T(8,128)(2,1)S(1)}, u32[]{:S(2)}, u32[]{:S(2)}) collective-permute-start(bf16[16,128,128]{2,1,0:T(8,128)(2,1)S(1)} %get-tuple-element.34), channel_id=1, source_target_pairs={{0,1},{1,0},{2,3},{3,2},{4,5},{5,4},{6,7},{7,6},{8,9},{9,8},{10,11... | collective-permute-start | bytes 1572872 | tf_op jit(solution)/shard_map/ppermute | solution.py:331
  217.9 4.1 %all-to-all-start.5 = ((bf16[16,256,128]{2,1,0:T(8,128)(2,1)}), bf16[16,256,128]{2,1,0:T(8,128)(2,1)S(1)}, u32[]{:S(2)}, u32[]{:S(2)}) async-start(bf16[16,256,128]{2,1,0:T(8,128)(2,1)} %shard_map.183), calls=%async_computation.5 | async-start | bytes 2097152 | tf_op jit(solution)/shard_map/all_to_all | solution.py:323
  223.3 4.8 %collective-permute-start.14 = (bf16[4,256,256]{2,1,0:T(8,128)(2,1)}, bf16[4,256,256]{2,1,0:T(8,128)(2,1)}, u32[]{:S(2)}, u32[]{:S(2)}) collective-permute-start(bf16[4,256,256]{2,1,0:T(8,128)(2,1)} %get-tuple-element.41), channel_id=1, source_target_pairs={{0,384},{32,416},{64,448},{96,480},{128,0},{160,32},{192,64},{224,... | collective-permute-start | bytes 1572872 | tf_op jit(solution)/shard_map/ppermute | solution.py:359
  235.8 4.3 %collective-permute-start.8 = (bf16[4,256,256]{2,1,0:T(8,128)(2,1)}, bf16[4,256,256]{2,1,0:T(8,128)(2,1)}, u32[]{:S(2)}, u32[]{:S(2)}) collective-permute-start(bf16[4,256,256]{2,1,0:T(8,128)(2,1)} %get-tuple-element.44), channel_id=1, source_target_pairs={{0,96},{32,0},{64,32},{96,64},{128,224},{160,128},{192,160},{224,1... | collective-permute-start | bytes 1572872 | tf_op jit(solution)/shard_map/ppermute | solution.py:359
  244.9 12.0 %collective-permute-done.12 = bf16[4,256,256]{2,1,0:T(8,128)(2,1)} collective-permute-done((bf16[4,256,256]{2,1,0:T(8,128)(2,1)}, bf16[4,256,256]{2,1,0:T(8,128)(2,1)}, u32[]{:S(2)}, u32[]{:S(2)}) %collective-permute-start.12) | collective-permute-done | bytes 524320 | tf_op jit(solution)/shard_map/ppermute | solution.py:359
  258.6 4.4 %collective-permute-start.17 = (bf16[256,256]{1,0:T(8,128)(2,1)S(1)}, bf16[256,256]{1,0:T(8,128)(2,1)S(1)}, u32[]{:S(2)}, u32[]{:S(2)}) collective-permute-start(bf16[256,256]{1,0:T(8,128)(2,1)S(1)} %get-tuple-element.47), channel_id=1, source_target_pairs={{0,96},{32,0},{64,32},{96,64},{128,224},{160,128},{192,160},{224,1... | collective-permute-start | bytes 393224 | tf_op jit(solution)/shard_map/ppermute | solution.py:359
  269.9 6.3 %collective-permute-start.11 = (bf16[256,256]{1,0:T(8,128)(2,1)S(1)}, bf16[256,256]{1,0:T(8,128)(2,1)S(1)}, u32[]{:S(2)}, u32[]{:S(2)}) collective-permute-start(bf16[256,256]{1,0:T(8,128)(2,1)S(1)} %get-tuple-element.50), channel_id=1, source_target_pairs={{0,384},{32,416},{64,448},{96,480},{128,0},{160,32},{192,64},{224,... | collective-permute-start | bytes 393224 | tf_op jit(solution)/shard_map/ppermute | solution.py:359
  276.3 3.0 %collective-permute-start.10 = (bf16[256,256]{1,0:T(8,128)(2,1)S(1)}, bf16[256,256]{1,0:T(8,128)(2,1)S(1)}, u32[]{:S(2)}, u32[]{:S(2)}) collective-permute-start(bf16[256,256]{1,0:T(8,128)(2,1)S(1)} %get-tuple-element.51), channel_id=1, source_target_pairs={{0,256},{32,288},{64,320},{96,352},{128,384},{160,416},{192,448},{... | collective-permute-start | bytes 393224 | tf_op jit(solution)/shard_map/ppermute | solution.py:359
  (117 shorter events, 70.2 us)
Async XLA Ops:
  9.6 51.2 %all-to-all-start = ((bf16[16,256,256]{2,1,0:T(8,128)(2,1)}), bf16[16,256,256]{2,1,0:T(8,128)(2,1)S(1)}, u32[]{:S(2)}, u32[]{:S(2)}) async-start(bf16[16,256,256]{2,1,0:T(8,128)(2,1)} %broadcast_in_dim.16), calls=%async_computation | async-start | bytes 4194304 | tf_op jit(solution)/shard_map/all_to_all | solution.py:323
  17.4 97.6 %all-gather.4.cloned.1.call-start = ((), (), s32[]{:S(2)}) async-start(), calls=%async_computation.6 | async-start | bytes 2228224 | tf_op jit(solution)/shard_map/all_gather | solution.py:369
  51.3 9.5 %collective-permute-start = (bf16[16,128,128]{2,1,0:T(8,128)(2,1)S(1)}, bf16[16,128,128]{2,1,0:T(8,128)(2,1)S(1)}, u32[]{:S(2)}, u32[]{:S(2)}) collective-permute-start(bf16[16,128,128]{2,1,0:T(8,128)(2,1)S(1)} %bitcast.52), channel_id=1, source_target_pairs={{0,1},{1,0},{2,3},{3,2},{4,5},{5,4},{6,7},{7,6},{8,9},{9,8},{10,11... | collective-permute-start | bytes 1572872 | tf_op jit(solution)/shard_map/ppermute | solution.py:331
  63.2 3.3 %collective-permute-start.1 = (bf16[128,544]{1,0:T(8,128)(2,1)S(1)}, bf16[128,544]{1,0:T(8,128)(2,1)S(1)}, u32[]{:S(2)}, u32[]{:S(2)}) collective-permute-start(bf16[128,544]{1,0:T(8,128)(2,1)S(1)} %get-tuple-element.21.mine_ref), channel_id=1, source_target_pairs={{0,1},{1,0},{2,3},{3,2},{4,5},{5,4},{6,7},{7,6},{8,9},{9,8},{10,11... | collective-permute-start | bytes 417800 | tf_op jit(solution)/shard_map/ppermute | solution.py:331
  108.4 14.2 %collective-permute-start.2 = (bf16[16,128,128]{2,1,0:T(8,128)(2,1)S(1)}, bf16[16,128,128]{2,1,0:T(8,128)(2,1)}, u32[]{:S(2)}, u32[]{:S(2)}) collective-permute-start(bf16[16,128,128]{2,1,0:T(8,128)(2,1)S(1)} %slice.12.mine_ref), channel_id=1, source_target_pairs={{0,1},{1,0},{2,3},{3,2},{4,5},{5,4},{6,7},{7,6},{8,9},{9,8},{10,11... | collective-permute-start | bytes 1572872 | tf_op jit(solution)/shard_map/ppermute | solution.py:331
  117.2 18.3 %all-to-all-start.2 = ((bf16[16,8,544]{2,1,0:T(8,128)(2,1)}), bf16[16,8,544]{2,1,0:T(8,128)(2,1)S(1)}, u32[]{:S(2)}, u32[]{:S(2)}) async-start(bf16[16,8,544]{2,1,0:T(8,128)(2,1)} %shard_map.174), calls=%async_computation.2 | async-start | bytes 327680 | tf_op jit(solution)/shard_map/all_to_all | solution.py:323
  147.4 5.0 %collective-permute-start.3 = (bf16[128,544]{1,0:T(8,128)(2,1)S(1)}, bf16[128,544]{1,0:T(8,128)(2,1)S(1)}, u32[]{:S(2)}, u32[]{:S(2)}) collective-permute-start(bf16[128,544]{1,0:T(8,128)(2,1)S(1)} %get-tuple-element.25.keep_ref), channel_id=1, source_target_pairs={{0,1},{1,0},{2,3},{3,2},{4,5},{5,4},{6,7},{7,6},{8,9},{9,8},{10,11... | collective-permute-start | bytes 417800 | tf_op jit(solution)/shard_map/ppermute | solution.py:331
  153.2 18.0 %all-to-all-start.3 = ((bf16[16,8,544]{2,1,0:T(8,128)(2,1)}), bf16[16,8,544]{2,1,0:T(8,128)(2,1)S(1)}, u32[]{:S(2)}, u32[]{:S(2)}) async-start(bf16[16,8,544]{2,1,0:T(8,128)(2,1)} %bitcast.7), calls=%async_computation.3 | async-start | bytes 327680 | tf_op jit(solution)/shard_map/all_to_all | solution.py:323
  174.5 20.0 %all-to-all-start.4 = ((bf16[16,8,544]{2,1,0:T(8,128)(2,1)}), bf16[16,8,544]{2,1,0:T(8,128)(2,1)}, u32[]{:S(2)}, u32[]{:S(2)}) async-start(bf16[16,8,544]{2,1,0:T(8,128)(2,1)} %copy-done.13), calls=%async_computation.4 | async-start | bytes 327680 | tf_op jit(solution)/shard_map/all_to_all | solution.py:323
  182.2 32.0 %collective-permute-start.4 = (bf16[16,128,128]{2,1,0:T(8,128)(2,1)}, bf16[16,128,128]{2,1,0:T(8,128)(2,1)}, u32[]{:S(2)}, u32[]{:S(2)}) collective-permute-start(bf16[16,128,128]{2,1,0:T(8,128)(2,1)} %copy-done.14), channel_id=1, source_target_pairs={{0,1},{1,0},{2,3},{3,2},{4,5},{5,4},{6,7},{7,6},{8,9},{9,8},{10,11... | collective-permute-start | bytes 1572872 | tf_op jit(solution)/shard_map/ppermute | solution.py:331
  208.0 7.7 %collective-permute-start.5 = (bf16[16,128,128]{2,1,0:T(8,128)(2,1)S(1)}, bf16[16,128,128]{2,1,0:T(8,128)(2,1)S(1)}, u32[]{:S(2)}, u32[]{:S(2)}) collective-permute-start(bf16[16,128,128]{2,1,0:T(8,128)(2,1)S(1)} %get-tuple-element.34), channel_id=1, source_target_pairs={{0,1},{1,0},{2,3},{3,2},{4,5},{5,4},{6,7},{7,6},{8,9},{9,8},{10,11... | collective-permute-start | bytes 1572872 | tf_op jit(solution)/shard_map/ppermute | solution.py:331
  217.9 69.1 %all-to-all-start.5 = ((bf16[16,256,128]{2,1,0:T(8,128)(2,1)}), bf16[16,256,128]{2,1,0:T(8,128)(2,1)S(1)}, u32[]{:S(2)}, u32[]{:S(2)}) async-start(bf16[16,256,128]{2,1,0:T(8,128)(2,1)} %shard_map.183), calls=%async_computation.5 | async-start | bytes 2097152 | tf_op jit(solution)/shard_map/all_to_all | solution.py:323
  223.3 19.2 %collective-permute-start.14 = (bf16[4,256,256]{2,1,0:T(8,128)(2,1)}, bf16[4,256,256]{2,1,0:T(8,128)(2,1)}, u32[]{:S(2)}, u32[]{:S(2)}) collective-permute-start(bf16[4,256,256]{2,1,0:T(8,128)(2,1)} %get-tuple-element.41), channel_id=1, source_target_pairs={{0,384},{32,416},{64,448},{96,480},{128,0},{160,32},{192,64},{224,... | collective-permute-start | bytes 1572872 | tf_op jit(solution)/shard_map/ppermute | solution.py:359
  228.1 16.8 %collective-permute-start.13 = (bf16[4,256,256]{2,1,0:T(8,128)(2,1)}, bf16[4,256,256]{2,1,0:T(8,128)(2,1)}, u32[]{:S(2)}, u32[]{:S(2)}) collective-permute-start(bf16[4,256,256]{2,1,0:T(8,128)(2,1)} %get-tuple-element.42), channel_id=1, source_target_pairs={{0,256},{32,288},{64,320},{96,352},{128,384},{160,416},{192,448},{... | collective-permute-start | bytes 1572872 | tf_op jit(solution)/shard_map/ppermute | solution.py:359
  230.7 26.2 %collective-permute-start.12 = (bf16[4,256,256]{2,1,0:T(8,128)(2,1)}, bf16[4,256,256]{2,1,0:T(8,128)(2,1)}, u32[]{:S(2)}, u32[]{:S(2)}) collective-permute-start(bf16[4,256,256]{2,1,0:T(8,128)(2,1)} %get-tuple-element.40), channel_id=1, source_target_pairs={{0,128},{32,160},{64,192},{96,224},{128,256},{160,288},{192,320},{... | collective-permute-start | bytes 1572872 | tf_op jit(solution)/shard_map/ppermute | solution.py:359
  235.8 29.8 %collective-permute-start.8 = (bf16[4,256,256]{2,1,0:T(8,128)(2,1)}, bf16[4,256,256]{2,1,0:T(8,128)(2,1)}, u32[]{:S(2)}, u32[]{:S(2)}) collective-permute-start(bf16[4,256,256]{2,1,0:T(8,128)(2,1)} %get-tuple-element.44), channel_id=1, source_target_pairs={{0,96},{32,0},{64,32},{96,64},{128,224},{160,128},{192,160},{224,1... | collective-permute-start | bytes 1572872 | tf_op jit(solution)/shard_map/ppermute | solution.py:359
  240.1 28.0 %collective-permute-start.7 = (bf16[4,256,256]{2,1,0:T(8,128)(2,1)}, bf16[4,256,256]{2,1,0:T(8,128)(2,1)}, u32[]{:S(2)}, u32[]{:S(2)}) collective-permute-start(bf16[4,256,256]{2,1,0:T(8,128)(2,1)} %get-tuple-element.45), channel_id=1, source_target_pairs={{0,64},{32,96},{64,0},{96,32},{128,192},{160,224},{192,128},{224,1... | collective-permute-start | bytes 1572872 | tf_op jit(solution)/shard_map/ppermute | solution.py:359
  242.5 25.6 %collective-permute-start.6 = (bf16[4,256,256]{2,1,0:T(8,128)(2,1)}, bf16[4,256,256]{2,1,0:T(8,128)(2,1)}, u32[]{:S(2)}, u32[]{:S(2)}) collective-permute-start(bf16[4,256,256]{2,1,0:T(8,128)(2,1)} %get-tuple-element.43), channel_id=1, source_target_pairs={{0,32},{32,64},{64,96},{96,0},{128,160},{160,192},{192,224},{224,1... | collective-permute-start | bytes 1572872 | tf_op jit(solution)/shard_map/ppermute | solution.py:359
  258.6 20.6 %collective-permute-start.17 = (bf16[256,256]{1,0:T(8,128)(2,1)S(1)}, bf16[256,256]{1,0:T(8,128)(2,1)S(1)}, u32[]{:S(2)}, u32[]{:S(2)}) collective-permute-start(bf16[256,256]{1,0:T(8,128)(2,1)S(1)} %get-tuple-element.47), channel_id=1, source_target_pairs={{0,96},{32,0},{64,32},{96,64},{128,224},{160,128},{192,160},{224,1... | collective-permute-start | bytes 393224 | tf_op jit(solution)/shard_map/ppermute | solution.py:359
  263.0 18.1 %collective-permute-start.16 = (bf16[256,256]{1,0:T(8,128)(2,1)S(1)}, bf16[256,256]{1,0:T(8,128)(2,1)S(1)}, u32[]{:S(2)}, u32[]{:S(2)}) collective-permute-start(bf16[256,256]{1,0:T(8,128)(2,1)S(1)} %get-tuple-element.48), channel_id=1, source_target_pairs={{0,64},{32,96},{64,0},{96,32},{128,192},{160,224},{192,128},{224,1... | collective-permute-start | bytes 393224 | tf_op jit(solution)/shard_map/ppermute | solution.py:359
  265.6 15.6 %collective-permute-start.15 = (bf16[256,256]{1,0:T(8,128)(2,1)S(1)}, bf16[256,256]{1,0:T(8,128)(2,1)S(1)}, u32[]{:S(2)}, u32[]{:S(2)}) collective-permute-start(bf16[256,256]{1,0:T(8,128)(2,1)S(1)} %get-tuple-element.46), channel_id=1, source_target_pairs={{0,32},{32,64},{64,96},{96,0},{128,160},{160,192},{192,224},{224,1... | collective-permute-start | bytes 393224 | tf_op jit(solution)/shard_map/ppermute | solution.py:359
  269.9 12.2 %collective-permute-start.11 = (bf16[256,256]{1,0:T(8,128)(2,1)S(1)}, bf16[256,256]{1,0:T(8,128)(2,1)S(1)}, u32[]{:S(2)}, u32[]{:S(2)}) collective-permute-start(bf16[256,256]{1,0:T(8,128)(2,1)S(1)} %get-tuple-element.50), channel_id=1, source_target_pairs={{0,384},{32,416},{64,448},{96,480},{128,0},{160,32},{192,64},{224,... | collective-permute-start | bytes 393224 | tf_op jit(solution)/shard_map/ppermute | solution.py:359
  276.3 7.2 %collective-permute-start.10 = (bf16[256,256]{1,0:T(8,128)(2,1)S(1)}, bf16[256,256]{1,0:T(8,128)(2,1)S(1)}, u32[]{:S(2)}, u32[]{:S(2)}) collective-permute-start(bf16[256,256]{1,0:T(8,128)(2,1)S(1)} %get-tuple-element.51), channel_id=1, source_target_pairs={{0,256},{32,288},{64,320},{96,352},{128,384},{160,416},{192,448},{... | collective-permute-start | bytes 393224 | tf_op jit(solution)/shard_map/ppermute | solution.py:359
  279.2 6.9 %collective-permute-start.9 = (bf16[256,256]{1,0:T(8,128)(2,1)S(1)}, bf16[256,256]{1,0:T(8,128)(2,1)S(1)}, u32[]{:S(2)}, u32[]{:S(2)}) collective-permute-start(bf16[256,256]{1,0:T(8,128)(2,1)S(1)} %get-tuple-element.49), channel_id=1, source_target_pairs={{0,128},{32,160},{64,192},{96,224},{128,256},{160,288},{192,320},{... | collective-permute-start | bytes 393224 | tf_op jit(solution)/shard_map/ppermute | solution.py:359
  (32 other events, 382.4 us)
Sparse Core Ops, SparseCore 0:
  21.2 65.4 all-gather.3
where the time goes:
time: 298 us; the launch traced here: 295 us
  starting transfers between devices  99.8 us (33%)
  blocking collectives  74.1 us (25%)
  waiting for transfers between devices  45.5 us (15%)
  Pallas kernels  32.1 us (11%)
  local copies, waits for them, and re-layouts  23.2 us (8%)
  between operations  14.7 us (5%)
  other arithmetic  5.36 us (2%)
    all_to_all x1, blocking collectives, exchange(): lax.all_to_all(parts, axis, split_axis=0, concat_axis=0, tiled=True, axis...  41 us
    ppermute x12, starting transfers between devices, to_owner(): total = total + lax.ppermute(entry(ahead), 'dp', perm).astype(f32)  39.5 us
    all_gather x1, blocking collectives, on_device(): mine = lax.all_gather(tokens, 'tensor', axis=0, axis_index_groups=ring)  33.2 us
    all_to_all x5, starting transfers between devices, exchange(): lax.all_to_all(parts, axis, split_axis=0, concat_axis=0, tiled=True, axis...  30.5 us
    ppermute x6, starting transfers between devices, other_core(): return lax.ppermute(value, 'tensor', swap)  29.8 us
    all_to_all x5, waiting for transfers between devices, exchange(): lax.all_to_all(parts, axis, split_axis=0, concat_axis=0, tiled=True, axis...  23.8 us
    unnamed x65, local copies, waits for them, and re-layouts  16.1 us
    ppermute x12, waiting for transfers between devices, to_owner(): total = total + lax.ppermute(entry(ahead), 'dp', perm).astype(f32)  16.1 us
  transfers between devices with their start and end apart: 24, of which 10 were waited for; matrix products, arithmetic and copies ran while one was open for 3% of the time, Pallas kernels for 6%

commit v1 on v0

--- a/solution.py
+++ b/solution.py
@@ -115,7 +115,7 @@
     refs[-1][...] = (keep_ref[...].astype(jnp.float32) + give_ref[...].astype(jnp.float32)).astype(jnp.bfloat16)
 
 
-def pairs_kernel(keep_out_ref, give_out_ref, keep_in_ref, give_in_ref, total_ref):
+def pairs_kernel(keep_out_ref, give_out_ref, keep_in_ref, give_in_ref, after_ref, total_ref):
     rows = keep_out_ref.shape[1]
     out = keep_out_ref[...] + give_out_ref[...].astype(jnp.float32)
     total_ref[:, :rows, :] = out.astype(jnp.bfloat16)
@@ -245,9 +245,10 @@
     lax.fori_loop(0, w_out_ref.shape[0], step, 0, unroll=2)
 
 
-def sign_in_kernel(
-    back_ref, low_ref, bc_ref, d_conv_ref, pre_ref, taps_ref, whole_ref, d_inner_ref, sign_ref
+def grad_kernel(
+    back_ref, low_ref, bc_ref, d_conv_ref, pre_ref, taps_ref, w_in_ref, even_ref, *refs
 ):
+    d_inner_ref, keep_ref, give_ref = refs[-3:]
     rank = low_ref.shape[1]
     back = back_ref[...]
     d_conv = (
@@ -269,16 +270,6 @@
     d_inner = d_inner.astype(jnp.bfloat16)
     d_inner_ref[...] = d_inner
 
-    def step(chip, carry):
-        side = sign_ref.shape[0]
-        sign_ref[lax.rem(chip, side), lax.div(chip, side)] = soft_sign(contract(whole_ref[chip], d_inner, 0, 0))
-        return carry
-
-    lax.fori_loop(0, whole_ref.shape[0], step, 0, unroll=2)
-
-
-def grad_kernel(d_inner_ref, w_in_ref, even_ref, keep_ref, give_ref):
-    d_inner = d_inner_ref[...]
     even = even_ref[...] > 0
 
     def step(chip, carry):
@@ -287,6 +278,18 @@
         return carry
 
     lax.fori_loop(0, w_in_ref.shape[0], step, 0, unroll=2)
+
+
+def sign_in_kernel(d_inner_ref, whole_ref, sign_ref):
+    d_inner = d_inner_ref[...]
+    side = sign_ref.shape[0]
+
+    def step(chip, carry):
+        sign = soft_sign(contract(whole_ref[chip], d_inner, 0, 0))
+        sign_ref[lax.rem(chip, side), lax.div(chip, side)] = sign
+        return carry
+
+    lax.fori_loop(0, whole_ref.shape[0], step, 0, unroll=2)
 
 
 def on_device(
@@ -338,12 +341,15 @@
         )(keep, other_core(give), *after)
         return total
 
-    def sum_channels(chip, *after):
+    def sum_shares(chip, *after):
         share = exchange(chip.reshape(chips, rows // chips, chip.shape[1]), "tensor", ring)
         (total,) = local_call(
             share_kernel, ((share.shape, bf16),), specs=[inside] + [left] * len(after)
         )(share, *after)
-        return exchange(total, "tensor", ring).reshape(chip.shape)
+        return total
+
+    def sum_channels(chip, *after):
+        return exchange(sum_shares(chip, *after), "tensor", ring).reshape(chip.shape)
 
     def to_owner(array, shift_of, stride):
         place = shift_of(lax.axis_index("dp"))
@@ -402,28 +408,34 @@
         + [pltpu.VMEM((rows + 1, a_log.shape[1], channels), f32)],
     )(small, w_dt, dt_bias[None, :], -jnp.exp(a_log).T, d_skip[None, :], conv_out, d_hidden)
     back_chip = pair_sum(back, back)
-    (sign_out,) = local_call(sign_out_kernel, (((chips, width, channels), bf16),), specs=[inside, inside, left])(
-        hidden_out, cot_whole, back_chip
-    )
+    (sign_out,) = local_call(
+        sign_out_kernel, (((chips, width, channels), bf16),), specs=[inside, inside, left]
+    )(hidden_out, cot_whole, back_chip)
+    votes_out = along_x(sign_out.reshape(side, side, width, channels)).astype(bf16)
+    total = sum_shares(back_chip, sign_out)
     out_parts = local_call(
         out_kernel,
         (((chips, rows, block), f32), ((chips, rows, block), bf16)),
         specs=[inside] * 3 + [left],
-    )(hidden_out, w_out_full, even, back_chip)
-    back = sum_channels(back_chip, sign_out, *out_parts)
-    d_inner, sign_in = local_call(
-        sign_in_kernel,
-        (((rows, channels), bf16), ((side, side, width, channels), bf16)),
-    )(back, w_dtlow, w_bc, d_conv, pre, conv_weight, whole)
+    )(hidden_out, w_out_full, even, total)
+    back = exchange(total, "tensor", ring).reshape(back_chip.shape)
+    d_inner, *grad_parts = local_call(
+        grad_kernel,
+        (
+            ((rows, channels), bf16),
+            ((chips, rows, block), f32),
+            ((chips, rows, block), bf16),
+        ),
+        specs=[inside] * 8 + [left] * 2,
+    )(back, w_dtlow, w_bc, d_conv, pre, conv_weight, w_in_full, even, votes_out, out_parts[0])
+    (sign_in,) = local_call(
+        sign_in_kernel, (((side, side, width, channels), bf16),), specs=[inside, inside]
+    )(d_inner, whole)
     votes_in = along_x(along_y(sign_in).astype(bf16))
-    votes_out = along_y(along_x(sign_out.reshape(side, side, width, channels)).astype(bf16))
-    grad_parts = local_call(
-        grad_kernel,
-        (((chips, rows, block), f32), ((chips, rows, block), bf16)),
-    )(d_inner, w_in_full, even)
-    (parts,) = local_call(pairs_kernel, (((chips, 2 * rows, block), bf16),))(
-        out_parts[0], other_core(out_parts[1]), grad_parts[0], other_core(grad_parts[1])
-    )
+    votes_out = along_y(votes_out)
+    (parts,) = local_call(
+        pairs_kernel, (((chips, 2 * rows, block), bf16),), specs=[inside] * 4 + [left]
+    )(out_parts[0], other_core(out_parts[1]), grad_parts[0], other_core(grad_parts[1]), sign_in)
     sums = jnp.sum(exchange(parts, "tensor", ring).astype(f32), axis=0).astype(bf16)
     merged_in = votes_in / replicas + err_in
     merged_out = votes_out / replicas + err_out

time: 298 us -> 289 us (0.970)
  waiting for transfers between devices: 45.5 us -> 34.4 us
  starting transfers between devices: 99.8 us -> 105 us
    all_to_all x5, waiting for transfers between devices: 23.8 us -> 9.15 us  [exchange(): lax.all_to_all(parts, axis, split_axis=0, concat_axis=0, tiled=True, axis...]
    all_to_all x5, starting transfers between devices: 30.5 us -> 37.2 us  [exchange(): lax.all_to_all(parts, axis, split_axis=0, concat_axis=0, tiled=True, axis...]
    ppermute x12, waiting for transfers between devices: 16.1 us -> 21.2 us  [to_owner(): total = total + lax.ppermute(entry(ahead), 'dp', perm).astype(f32)]
    ppermute x12, starting transfers between devices: 39.5 us -> 36.3 us  [to_owner(): total = total + lax.ppermute(entry(ahead), 'dp', perm).astype(f32)]
    unnamed x65 -> x79, local copies, waits for them, and re-layouts: 16.1 us -> 14.8 us
  transfers between devices with their start and end apart: 24 -> 24, of which waited for: 10 -> 10; matrix products, arithmetic and copies ran while one was open for 3% -> 3% of each run, Pallas kernels for 6% -> 7%
where the time goes in v1:
time: 289 us; the launch traced here: 287 us
  starting transfers between devices  105 us (36%)
  blocking collectives  74.2 us (26%)
  waiting for transfers between devices  34.4 us (12%)
  Pallas kernels  31.6 us (11%)
  local copies, waits for them, and re-layouts  20.4 us (7%)
  between operations  14.8 us (5%)
  other arithmetic  6.58 us (2%)
    all_to_all x1, blocking collectives, exchange(): lax.all_to_all(parts, axis, split_axis=0, concat_axis=0, tiled=True, axis...  41 us
    all_to_all x5, starting transfers between devices, exchange(): lax.all_to_all(parts, axis, split_axis=0, concat_axis=0, tiled=True, axis...  37.2 us
    ppermute x12, starting transfers between devices, to_owner(): total = total + lax.ppermute(entry(ahead), 'dp', perm).astype(f32)  36.3 us
    all_gather x1, blocking collectives, on_device(): mine = lax.all_gather(tokens, 'tensor', axis=0, axis_index_groups=ring)  33.2 us
    ppermute x6, starting transfers between devices, other_core(): return lax.ppermute(value, 'tensor', swap)  31.4 us
    ppermute x12, waiting for transfers between devices, to_owner(): total = total + lax.ppermute(entry(ahead), 'dp', perm).astype(f32)  21.2 us
    unnamed x79, local copies, waits for them, and re-layouts  14.8 us
    pallas_call x1, Pallas kernels, on_device(): local_call(scan_kernel, (((rows, channels), bf16), ((rows, channels), f32...  11 us
  transfers between devices with their start and end apart: 24, of which 10 were waited for; matrix products, arithmetic and copies ran while one was open for 3% of the time, Pallas kernels for 7%

profile of v1, /device:TPU:1, one launch (start us, length us, event | category | flops | bytes accessed | tf_op | source)
XLA Modules:
  0.0 287.0 jit_solution(10901476759034475662)
XLA Ops:
  9.6 7.7 %all-to-all-start = ((bf16[16,256,256]{2,1,0:T(8,128)(2,1)}), bf16[16,256,256]{2,1,0:T(8,128)(2,1)S(1)}, u32[]{:S(2)}, u32[]{:S(2)}) async-start(bf16[16,256,256]{2,1,0:T(8,128)(2,1)} %broadcast_in_dim.16), calls=%async_computation | async-start | bytes 4194304 | tf_op jit(solution)/shard_map/all_to_all | solution.py:326
  18.1 33.2 %all-gather = bf16[2048,128]{1,0:T(8,128)(2,1)S(1)} all-gather(bf16[128,128]{1,0:T(8,128)(2,1)S(1)} %copy-done.36), channel_id=2, replica_groups={{0,2,4,6,8,10,12,14,16,18,20,22,24,26,28,30},{1,3,5,7,9,11,13,15,17,19,..., dimensions={0}, use_global_device_ids=true | all-gather | bytes 557056 | tf_op jit(solution)/shard_map/all_gather | solution.py:376
  51.3 8.0 %collective-permute-start = (bf16[16,128,128]{2,1,0:T(8,128)(2,1)S(1)}, bf16[16,128,128]{2,1,0:T(8,128)(2,1)S(1)}, u32[]{:S(2)}, u32[]{:S(2)}) collective-permute-start(bf16[16,128,128]{2,1,0:T(8,128)(2,1)S(1)} %bitcast.52), channel_id=1, source_target_pairs={{0,1},{1,0},{2,3},{3,2},{4,5},{5,4},{6,7},{7,6},{8,9},{9,8},{10,11... | collective-permute-start | bytes 1572872 | tf_op jit(solution)/shard_map/ppermute | solution.py:334
  66.6 41.0 %all_to_all.30.parts_ref = bf16[16,176,128]{2,1,0:T(8,128)(2,1)S(1)} all-to-all(bf16[16,176,128]{2,1,0:T(8,128)(2,1)S(1)} %shard_map.173), channel_id=1, replica_groups={{0,2,4,6,8,10,12,14,16,18,20,22,24,26,28,30},{1,3,5,7,9,11,13,15,17,19,..., dimensions={0} | all-to-all | bytes 1441792 | tf_op jit(solution)/shard_map/all_to_all | solution.py:326
  107.7 6.5 %collective-permute-start.2 = (bf16[16,128,128]{2,1,0:T(8,128)(2,1)S(1)}, bf16[16,128,128]{2,1,0:T(8,128)(2,1)}, u32[]{:S(2)}, u32[]{:S(2)}) collective-permute-start(bf16[16,128,128]{2,1,0:T(8,128)(2,1)S(1)} %slice.12.mine_ref), channel_id=1, source_target_pairs={{0,1},{1,0},{2,3},{3,2},{4,5},{5,4},{6,7},{7,6},{8,9},{9,8},{10,11... | collective-permute-start | bytes 1572872 | tf_op jit(solution)/shard_map/ppermute | solution.py:334
  116.5 5.4 %all-to-all-start.2 = ((bf16[16,8,544]{2,1,0:T(8,128)(2,1)}), bf16[16,8,544]{2,1,0:T(8,128)(2,1)S(1)}, u32[]{:S(2)}, u32[]{:S(2)}) async-start(bf16[16,8,544]{2,1,0:T(8,128)(2,1)} %shard_map.174), calls=%async_computation.2 | async-start | bytes 327680 | tf_op jit(solution)/shard_map/all_to_all | solution.py:326
  125.9 8.8 %all-to-all-done.2 = bf16[16,8,544]{2,1,0:T(8,128)(2,1)S(1)} async-done(((bf16[16,8,544]{2,1,0:T(8,128)(2,1)}), bf16[16,8,544]{2,1,0:T(8,128)(2,1)S(1)}, u32[]{:S(2)}, u32[]{:S(2)}) %all-to-all-start.2) | async-done | bytes 139296 | tf_op jit(solution)/shard_map/all_to_all | solution.py:326
  137.6 11.0 %shard_map.176 = (bf16[128,256]{1,0:T(8,128)(2,1)S(1)}, f32[128,256]{1,0:T(8,128)S(1)}, bf16[128,544]{1,0:T(8,128)(2,1)S(1)}) custom-call(bf16[128,544]{1,0:T(8,128)(2,1)S(1)} %bitcast.55, bf16[512,256]{1,0:T(8,128)(2,1)S(1)} %copy-done.21, f32[1,256]{1,0:T(1,128)S(1)} %bitcast.56, f32[16,256]{1,0:T(8,128)S(1)} %negate_bitcast_fusion.a_neg_ref, ...), custom_call_target="tpu_custom_call" | custom-call | tf_op jit(solution)/shard_map/pallas_call | solution.py:404
  149.2 4.0 %collective-permute-start.3 = (bf16[128,544]{1,0:T(8,128)(2,1)S(1)}, bf16[128,544]{1,0:T(8,128)(2,1)S(1)}, u32[]{:S(2)}, u32[]{:S(2)}) collective-permute-start(bf16[128,544]{1,0:T(8,128)(2,1)S(1)} %get-tuple-element.24.keep_ref), channel_id=1, source_target_pairs={{0,1},{1,0},{2,3},{3,2},{4,5},{5,4},{6,7},{7,6},{8,9},{9,8},{10,11... | collective-permute-start | bytes 417800 | tf_op jit(solution)/shard_map/ppermute | solution.py:334
  154.9 5.6 %all-to-all-start.3 = ((bf16[16,8,544]{2,1,0:T(8,128)(2,1)}), bf16[16,8,544]{2,1,0:T(8,128)(2,1)S(1)}, u32[]{:S(2)}, u32[]{:S(2)}) async-start(bf16[16,8,544]{2,1,0:T(8,128)(2,1)} %bitcast.7), calls=%async_computation.3 | async-start | bytes 327680 | tf_op jit(solution)/shard_map/all_to_all | solution.py:326
  161.4 3.3 %shard_map.178.refs_0_ = bf16[16,256,256]{2,1,0:T(8,128)(2,1)S(1)} custom-call(bf16[128,256]{1,0:T(8,128)(2,1)S(1)} %copy-done.19, bf16[16,128,256]{2,1,0:T(8,128)(2,1)S(1)} %copy-done.13, bf16[128,544]{1,0:T(8,128)(2,1)} %shard_map.177.after_ref), custom_call_target="tpu_custom_call" | custom-call | tf_op jit(solution)/shard_map/pallas_call | solution.py:411
  167.4 4.8 %collective-permute-start.7 = (bf16[4,256,256]{2,1,0:T(8,128)(2,1)}, bf16[4,256,256]{2,1,0:T(8,128)(2,1)}, u32[]{:S(2)}, u32[]{:S(2)}) collective-permute-start(bf16[4,256,256]{2,1,0:T(8,128)(2,1)} %get-tuple-element.42), channel_id=1, source_target_pairs={{0,384},{32,416},{64,448},{96,480},{128,0},{160,32},{192,64},{224,... | collective-permute-start | bytes 1572872 | tf_op jit(solution)/shard_map/ppermute | solution.py:365
  179.5 11.4 %all-to-all-start.4 = ((bf16[16,8,544]{2,1,0:T(8,128)(2,1)}), bf16[16,8,544]{2,1,0:T(8,128)(2,1)S(1)}, u32[]{:S(2)}, u32[]{:S(2)}) async-start(bf16[16,8,544]{2,1,0:T(8,128)(2,1)} %shard_map.179.after_ref), calls=%async_computation.4 | async-start | bytes 327680 | tf_op jit(solution)/shard_map/all_to_all | solution.py:326
  191.0 3.5 %shard_map.180 = (f32[16,128,128]{2,1,0:T(8,128)S(1)}, bf16[16,128,128]{2,1,0:T(8,128)(2,1)}) custom-call(bf16[128,256]{1,0:T(8,128)(2,1)S(1)} %copy-done.20, bf16[16,256,256]{2,1,0:T(8,128)(2,1)S(1)} %bitcast.49, s32[1,1]{1,0:T(1,128)} %bitcast.1.even_ref, bf16[16,8,544]{2,1,0:T(8,128)(2,1)} %shard_map.179.after_ref), custom_call_target="tpu_custom_call" | custom-call | tf_op jit(solution)/shard_map/pallas_call | solution.py:416
  195.5 4.1 %collective-permute-start.4 = (bf16[16,128,128]{2,1,0:T(8,128)(2,1)}, bf16[16,128,128]{2,1,0:T(8,128)(2,1)}, u32[]{:S(2)}, u32[]{:S(2)}) collective-permute-start(bf16[16,128,128]{2,1,0:T(8,128)(2,1)} %get-tuple-element.27), channel_id=1, source_target_pairs={{0,1},{1,0},{2,3},{3,2},{4,5},{5,4},{6,7},{7,6},{8,9},{9,8},{10,11... | collective-permute-start | bytes 1572872 | tf_op jit(solution)/shard_map/ppermute | solution.py:334
  204.3 3.3 %shard_map.181 = (bf16[128,256]{1,0:T(8,128)(2,1)S(1)}, f32[16,128,128]{2,1,0:T(8,128)S(1)}, bf16[16,128,128]{2,1,0:T(8,128)(2,1)S(1)}) custom-call(bf16[128,544]{1,0:T(8,128)(2,1)S(1)} %bitcast.54, bf16[256,512]{1,0:T(8,128)(2,1)S(1)} %copy-done.15, bf16[256,32]{1,0:T(8,128)(2,1)S(1)} %copy-done.17, f32[128,256]{1,0:T(8,128)S(1)} %copy-done.25, ...), custom_call_target="tpu_custom_call" | custom-call | tf_op jit(solution)/shard_map/pallas_call | solution.py:422
  207.7 6.6 %collective-permute-start.8 = (bf16[16,128,128]{2,1,0:T(8,128)(2,1)S(1)}, bf16[16,128,128]{2,1,0:T(8,128)(2,1)S(1)}, u32[]{:S(2)}, u32[]{:S(2)}) collective-permute-start(bf16[16,128,128]{2,1,0:T(8,128)(2,1)S(1)} %get-tuple-element.31), channel_id=1, source_target_pairs={{0,1},{1,0},{2,3},{3,2},{4,5},{5,4},{6,7},{7,6},{8,9},{9,8},{10,11... | collective-permute-start | bytes 1572872 | tf_op jit(solution)/shard_map/ppermute | solution.py:334
  214.2 3.4 %shard_map.182.after_ref = bf16[4,4,256,256]{3,2,1,0:T(8,128)(2,1)S(1)} custom-call(bf16[128,256]{1,0:T(8,128)(2,1)S(1)} %get-tuple-element.32.d_inner_ref, bf16[16,128,256]{2,1,0:T(8,128)(2,1)S(1)} %copy-done.11), custom_call_target="tpu_custom_call" | custom-call | tf_op jit(solution)/shard_map/pallas_call | solution.py:431
  219.9 7.1 %all-to-all-start.5 = ((bf16[16,256,128]{2,1,0:T(8,128)(2,1)}), bf16[16,256,128]{2,1,0:T(8,128)(2,1)}, u32[]{:S(2)}, u32[]{:S(2)}) async-start(bf16[16,256,128]{2,1,0:T(8,128)(2,1)} %copy-done.6), calls=%async_computation.5 | async-start | bytes 2097152 | tf_op jit(solution)/shard_map/all_to_all | solution.py:326
  228.2 4.3 %collective-permute-start.11 = (bf16[4,256,256]{2,1,0:T(8,128)(2,1)}, bf16[4,256,256]{2,1,0:T(8,128)(2,1)}, u32[]{:S(2)}, u32[]{:S(2)}) collective-permute-start(bf16[4,256,256]{2,1,0:T(8,128)(2,1)} %get-tuple-element.39), channel_id=1, source_target_pairs={{0,96},{32,0},{64,32},{96,64},{128,224},{160,128},{192,160},{224,1... | collective-permute-start | bytes 1572872 | tf_op jit(solution)/shard_map/ppermute | solution.py:365
  237.4 4.2 %collective-permute-start.17 = (bf16[256,256]{1,0:T(8,128)(2,1)S(1)}, bf16[256,256]{1,0:T(8,128)(2,1)S(1)}, u32[]{:S(2)}, u32[]{:S(2)}) collective-permute-start(bf16[256,256]{1,0:T(8,128)(2,1)S(1)} %get-tuple-element.45), channel_id=1, source_target_pairs={{0,96},{32,0},{64,32},{96,64},{128,224},{160,128},{192,160},{224,1... | collective-permute-start | bytes 393224 | tf_op jit(solution)/shard_map/ppermute | solution.py:365
  244.8 9.5 %collective-permute-done.11 = bf16[4,256,256]{2,1,0:T(8,128)(2,1)} collective-permute-done((bf16[4,256,256]{2,1,0:T(8,128)(2,1)}, bf16[4,256,256]{2,1,0:T(8,128)(2,1)}, u32[]{:S(2)}, u32[]{:S(2)}) %collective-permute-start.11) | collective-permute-done | bytes 524320 | tf_op jit(solution)/shard_map/ppermute | solution.py:365
  256.3 5.8 %collective-permute-done.9 = bf16[4,256,256]{2,1,0:T(8,128)(2,1)} collective-permute-done((bf16[4,256,256]{2,1,0:T(8,128)(2,1)S(1)}, bf16[4,256,256]{2,1,0:T(8,128)(2,1)}, u32[]{:S(2)}, u32[]{:S(2)}) %collective-permute-start.9) | collective-permute-done | bytes 524320 | tf_op jit(solution)/shard_map/ppermute | solution.py:365
  266.7 3.2 %collective-permute-start.13 = (bf16[256,256]{1,0:T(8,128)(2,1)S(1)}, bf16[256,256]{1,0:T(8,128)(2,1)S(1)}, u32[]{:S(2)}, u32[]{:S(2)}) collective-permute-start(bf16[256,256]{1,0:T(8,128)(2,1)S(1)} %get-tuple-element.49), channel_id=1, source_target_pairs={{0,256},{32,288},{64,320},{96,352},{128,384},{160,416},{192,448},{... | collective-permute-start | bytes 393224 | tf_op jit(solution)/shard_map/ppermute | solution.py:365
  (131 shorter events, 66.5 us)
Async XLA Ops:
  9.6 51.2 %all-to-all-start = ((bf16[16,256,256]{2,1,0:T(8,128)(2,1)}), bf16[16,256,256]{2,1,0:T(8,128)(2,1)S(1)}, u32[]{:S(2)}, u32[]{:S(2)}) async-start(bf16[16,256,256]{2,1,0:T(8,128)(2,1)} %broadcast_in_dim.16), calls=%async_computation | async-start | bytes 4194304 | tf_op jit(solution)/shard_map/all_to_all | solution.py:326
  17.3 96.8 %all-gather.4.cloned.1.call-start = ((), (), s32[]{:S(2)}) async-start(), calls=%async_computation.6 | async-start | bytes 2228224 | tf_op jit(solution)/shard_map/all_gather | solution.py:375
  51.3 9.5 %collective-permute-start = (bf16[16,128,128]{2,1,0:T(8,128)(2,1)S(1)}, bf16[16,128,128]{2,1,0:T(8,128)(2,1)S(1)}, u32[]{:S(2)}, u32[]{:S(2)}) collective-permute-start(bf16[16,128,128]{2,1,0:T(8,128)(2,1)S(1)} %bitcast.52), channel_id=1, source_target_pairs={{0,1},{1,0},{2,3},{3,2},{4,5},{5,4},{6,7},{7,6},{8,9},{9,8},{10,11... | collective-permute-start | bytes 1572872 | tf_op jit(solution)/shard_map/ppermute | solution.py:334
  63.2 3.3 %collective-permute-start.1 = (bf16[128,544]{1,0:T(8,128)(2,1)S(1)}, bf16[128,544]{1,0:T(8,128)(2,1)S(1)}, u32[]{:S(2)}, u32[]{:S(2)}) collective-permute-start(bf16[128,544]{1,0:T(8,128)(2,1)S(1)} %get-tuple-element.20.mine_ref), channel_id=1, source_target_pairs={{0,1},{1,0},{2,3},{3,2},{4,5},{5,4},{6,7},{7,6},{8,9},{9,8},{10,11... | collective-permute-start | bytes 417800 | tf_op jit(solution)/shard_map/ppermute | solution.py:334
  107.7 14.2 %collective-permute-start.2 = (bf16[16,128,128]{2,1,0:T(8,128)(2,1)S(1)}, bf16[16,128,128]{2,1,0:T(8,128)(2,1)}, u32[]{:S(2)}, u32[]{:S(2)}) collective-permute-start(bf16[16,128,128]{2,1,0:T(8,128)(2,1)S(1)} %slice.12.mine_ref), channel_id=1, source_target_pairs={{0,1},{1,0},{2,3},{3,2},{4,5},{5,4},{6,7},{7,6},{8,9},{9,8},{10,11... | collective-permute-start | bytes 1572872 | tf_op jit(solution)/shard_map/ppermute | solution.py:334
  116.5 18.3 %all-to-all-start.2 = ((bf16[16,8,544]{2,1,0:T(8,128)(2,1)}), bf16[16,8,544]{2,1,0:T(8,128)(2,1)S(1)}, u32[]{:S(2)}, u32[]{:S(2)}) async-start(bf16[16,8,544]{2,1,0:T(8,128)(2,1)} %shard_map.174), calls=%async_computation.2 | async-start | bytes 327680 | tf_op jit(solution)/shard_map/all_to_all | solution.py:326
  149.2 5.0 %collective-permute-start.3 = (bf16[128,544]{1,0:T(8,128)(2,1)S(1)}, bf16[128,544]{1,0:T(8,128)(2,1)S(1)}, u32[]{:S(2)}, u32[]{:S(2)}) collective-permute-start(bf16[128,544]{1,0:T(8,128)(2,1)S(1)} %get-tuple-element.24.keep_ref), channel_id=1, source_target_pairs={{0,1},{1,0},{2,3},{3,2},{4,5},{5,4},{6,7},{7,6},{8,9},{9,8},{10,11... | collective-permute-start | bytes 417800 | tf_op jit(solution)/shard_map/ppermute | solution.py:334
  154.9 22.3 %all-to-all-start.3 = ((bf16[16,8,544]{2,1,0:T(8,128)(2,1)}), bf16[16,8,544]{2,1,0:T(8,128)(2,1)S(1)}, u32[]{:S(2)}, u32[]{:S(2)}) async-start(bf16[16,8,544]{2,1,0:T(8,128)(2,1)} %bitcast.7), calls=%async_computation.3 | async-start | bytes 327680 | tf_op jit(solution)/shard_map/all_to_all | solution.py:326
  167.4 32.2 %collective-permute-start.7 = (bf16[4,256,256]{2,1,0:T(8,128)(2,1)}, bf16[4,256,256]{2,1,0:T(8,128)(2,1)}, u32[]{:S(2)}, u32[]{:S(2)}) collective-permute-start(bf16[4,256,256]{2,1,0:T(8,128)(2,1)} %get-tuple-element.42), channel_id=1, source_target_pairs={{0,384},{32,416},{64,448},{96,480},{128,0},{160,32},{192,64},{224,... | collective-permute-start | bytes 1572872 | tf_op jit(solution)/shard_map/ppermute | solution.py:365
  172.2 27.4 %collective-permute-start.6 = (bf16[4,256,256]{2,1,0:T(8,128)(2,1)}, bf16[4,256,256]{2,1,0:T(8,128)(2,1)}, u32[]{:S(2)}, u32[]{:S(2)}) collective-permute-start(bf16[4,256,256]{2,1,0:T(8,128)(2,1)} %get-tuple-element.43), channel_id=1, source_target_pairs={{0,256},{32,288},{64,320},{96,352},{128,384},{160,416},{192,448},{... | collective-permute-start | bytes 1572872 | tf_op jit(solution)/shard_map/ppermute | solution.py:365
  174.8 26.2 %collective-permute-start.5 = (bf16[4,256,256]{2,1,0:T(8,128)(2,1)}, bf16[4,256,256]{2,1,0:T(8,128)(2,1)}, u32[]{:S(2)}, u32[]{:S(2)}) collective-permute-start(bf16[4,256,256]{2,1,0:T(8,128)(2,1)} %get-tuple-element.41), channel_id=1, source_target_pairs={{0,128},{32,160},{64,192},{96,224},{128,256},{160,288},{192,320},{... | collective-permute-start | bytes 1572872 | tf_op jit(solution)/shard_map/ppermute | solution.py:365
  179.5 23.6 %all-to-all-start.4 = ((bf16[16,8,544]{2,1,0:T(8,128)(2,1)}), bf16[16,8,544]{2,1,0:T(8,128)(2,1)S(1)}, u32[]{:S(2)}, u32[]{:S(2)}) async-start(bf16[16,8,544]{2,1,0:T(8,128)(2,1)} %shard_map.179.after_ref), calls=%async_computation.4 | async-start | bytes 327680 | tf_op jit(solution)/shard_map/all_to_all | solution.py:326
  195.5 22.1 %collective-permute-start.4 = (bf16[16,128,128]{2,1,0:T(8,128)(2,1)}, bf16[16,128,128]{2,1,0:T(8,128)(2,1)}, u32[]{:S(2)}, u32[]{:S(2)}) collective-permute-start(bf16[16,128,128]{2,1,0:T(8,128)(2,1)} %get-tuple-element.27), channel_id=1, source_target_pairs={{0,1},{1,0},{2,3},{3,2},{4,5},{5,4},{6,7},{7,6},{8,9},{9,8},{10,11... | collective-permute-start | bytes 1572872 | tf_op jit(solution)/shard_map/ppermute | solution.py:334
  207.7 10.0 %collective-permute-start.8 = (bf16[16,128,128]{2,1,0:T(8,128)(2,1)S(1)}, bf16[16,128,128]{2,1,0:T(8,128)(2,1)S(1)}, u32[]{:S(2)}, u32[]{:S(2)}) collective-permute-start(bf16[16,128,128]{2,1,0:T(8,128)(2,1)S(1)} %get-tuple-element.31), channel_id=1, source_target_pairs={{0,1},{1,0},{2,3},{3,2},{4,5},{5,4},{6,7},{7,6},{8,9},{9,8},{10,11... | collective-permute-start | bytes 1572872 | tf_op jit(solution)/shard_map/ppermute | solution.py:334
  219.9 58.3 %all-to-all-start.5 = ((bf16[16,256,128]{2,1,0:T(8,128)(2,1)}), bf16[16,256,128]{2,1,0:T(8,128)(2,1)}, u32[]{:S(2)}, u32[]{:S(2)}) async-start(bf16[16,256,128]{2,1,0:T(8,128)(2,1)} %copy-done.6), calls=%async_computation.5 | async-start | bytes 2097152 | tf_op jit(solution)/shard_map/all_to_all | solution.py:326
  228.2 26.1 %collective-permute-start.11 = (bf16[4,256,256]{2,1,0:T(8,128)(2,1)}, bf16[4,256,256]{2,1,0:T(8,128)(2,1)}, u32[]{:S(2)}, u32[]{:S(2)}) collective-permute-start(bf16[4,256,256]{2,1,0:T(8,128)(2,1)} %get-tuple-element.39), channel_id=1, source_target_pairs={{0,96},{32,0},{64,32},{96,64},{128,224},{160,128},{192,160},{224,1... | collective-permute-start | bytes 1572872 | tf_op jit(solution)/shard_map/ppermute | solution.py:365
  232.5 23.8 %collective-permute-start.10 = (bf16[4,256,256]{2,1,0:T(8,128)(2,1)}, bf16[4,256,256]{2,1,0:T(8,128)(2,1)}, u32[]{:S(2)}, u32[]{:S(2)}) collective-permute-start(bf16[4,256,256]{2,1,0:T(8,128)(2,1)} %get-tuple-element.40), channel_id=1, source_target_pairs={{0,64},{32,96},{64,0},{96,32},{128,192},{160,224},{192,128},{224,1... | collective-permute-start | bytes 1572872 | tf_op jit(solution)/shard_map/ppermute | solution.py:365
  234.9 27.2 %collective-permute-start.9 = (bf16[4,256,256]{2,1,0:T(8,128)(2,1)S(1)}, bf16[4,256,256]{2,1,0:T(8,128)(2,1)}, u32[]{:S(2)}, u32[]{:S(2)}) collective-permute-start(bf16[4,256,256]{2,1,0:T(8,128)(2,1)S(1)} %get-tuple-element.38), channel_id=1, source_target_pairs={{0,32},{32,64},{64,96},{96,0},{128,160},{160,192},{192,224},{224,1... | collective-permute-start | bytes 1572872 | tf_op jit(solution)/shard_map/ppermute | solution.py:365
  237.4 32.5 %collective-permute-start.17 = (bf16[256,256]{1,0:T(8,128)(2,1)S(1)}, bf16[256,256]{1,0:T(8,128)(2,1)S(1)}, u32[]{:S(2)}, u32[]{:S(2)}) collective-permute-start(bf16[256,256]{1,0:T(8,128)(2,1)S(1)} %get-tuple-element.45), channel_id=1, source_target_pairs={{0,96},{32,0},{64,32},{96,64},{128,224},{160,128},{192,160},{224,1... | collective-permute-start | bytes 393224 | tf_op jit(solution)/shard_map/ppermute | solution.py:365
  241.7 30.2 %collective-permute-start.16 = (bf16[256,256]{1,0:T(8,128)(2,1)S(1)}, bf16[256,256]{1,0:T(8,128)(2,1)S(1)}, u32[]{:S(2)}, u32[]{:S(2)}) collective-permute-start(bf16[256,256]{1,0:T(8,128)(2,1)S(1)} %get-tuple-element.46), channel_id=1, source_target_pairs={{0,64},{32,96},{64,0},{96,32},{128,192},{160,224},{192,128},{224,1... | collective-permute-start | bytes 393224 | tf_op jit(solution)/shard_map/ppermute | solution.py:365
  254.2 17.6 %collective-permute-start.15 = (bf16[256,256]{1,0:T(8,128)(2,1)S(1)}, bf16[256,256]{1,0:T(8,128)(2,1)S(1)}, u32[]{:S(2)}, u32[]{:S(2)}) collective-permute-start(bf16[256,256]{1,0:T(8,128)(2,1)S(1)} %get-tuple-element.44), channel_id=1, source_target_pairs={{0,32},{32,64},{64,96},{96,0},{128,160},{160,192},{192,224},{224,1... | collective-permute-start | bytes 393224 | tf_op jit(solution)/shard_map/ppermute | solution.py:365
  263.8 9.0 %collective-permute-start.14 = (bf16[256,256]{1,0:T(8,128)(2,1)S(1)}, bf16[256,256]{1,0:T(8,128)(2,1)S(1)}, u32[]{:S(2)}, u32[]{:S(2)}) collective-permute-start(bf16[256,256]{1,0:T(8,128)(2,1)S(1)} %get-tuple-element.48), channel_id=1, source_target_pairs={{0,384},{32,416},{64,448},{96,480},{128,0},{160,32},{192,64},{224,... | collective-permute-start | bytes 393224 | tf_op jit(solution)/shard_map/ppermute | solution.py:365
  266.7 7.6 %collective-permute-start.13 = (bf16[256,256]{1,0:T(8,128)(2,1)S(1)}, bf16[256,256]{1,0:T(8,128)(2,1)S(1)}, u32[]{:S(2)}, u32[]{:S(2)}) collective-permute-start(bf16[256,256]{1,0:T(8,128)(2,1)S(1)} %get-tuple-element.49), channel_id=1, source_target_pairs={{0,256},{32,288},{64,320},{96,352},{128,384},{160,416},{192,448},{... | collective-permute-start | bytes 393224 | tf_op jit(solution)/shard_map/ppermute | solution.py:365
  269.9 7.3 %collective-permute-start.12 = (bf16[256,256]{1,0:T(8,128)(2,1)S(1)}, bf16[256,256]{1,0:T(8,128)(2,1)S(1)}, u32[]{:S(2)}, u32[]{:S(2)}) collective-permute-start(bf16[256,256]{1,0:T(8,128)(2,1)S(1)} %get-tuple-element.47), channel_id=1, source_target_pairs={{0,128},{32,160},{64,192},{96,224},{128,256},{160,288},{192,320},{... | collective-permute-start | bytes 393224 | tf_op jit(solution)/shard_map/ppermute | solution.py:365
  (39 other events, 573.9 us)
Sparse Core Ops, SparseCore 0:
  21.2 65.4 all-gather.3

commit v2 on v1

--- a/solution.py
+++ b/solution.py
@@ -286,7 +286,7 @@
 
     def step(chip, carry):
         sign = soft_sign(contract(whole_ref[chip], d_inner, 0, 0))
-        sign_ref[lax.rem(chip, side), lax.div(chip, side)] = sign
+        sign_ref[lax.div(chip, side), lax.rem(chip, side)] = sign
         return carry
 
     lax.fori_loop(0, whole_ref.shape[0], step, 0, unroll=2)
@@ -431,7 +431,7 @@
     (sign_in,) = local_call(
         sign_in_kernel, (((side, side, width, channels), bf16),), specs=[inside, inside]
     )(d_inner, whole)
-    votes_in = along_x(along_y(sign_in).astype(bf16))
+    votes_in = along_y(along_x(sign_in).astype(bf16))
     votes_out = along_y(votes_out)
     (parts,) = local_call(
         pairs_kernel, (((chips, 2 * rows, block), bf16),), specs=[inside] * 4 + [left]

time: 289 us -> 288 us (level)
  no operation moved by 1% of the time
where the time goes in v2:
time: 288 us; the launch traced here: 286 us
  starting transfers between devices  105 us (36%)
  blocking collectives  74.2 us (26%)
  waiting for transfers between devices  33.4 us (12%)
  Pallas kernels  31.6 us (11%)
  local copies, waits for them, and re-layouts  20.4 us (7%)
  between operations  14.8 us (5%)
  other arithmetic  6.58 us (2%)
    all_to_all x1, blocking collectives, exchange(): lax.all_to_all(parts, axis, split_axis=0, concat_axis=0, tiled=True, axis...  41 us
    all_to_all x5, starting transfers between devices, exchange(): lax.all_to_all(parts, axis, split_axis=0, concat_axis=0, tiled=True, axis...  37.2 us
    ppermute x12, starting transfers between devices, to_owner(): total = total + lax.ppermute(entry(ahead), 'dp', perm).astype(f32)  36.5 us
    all_gather x1, blocking collectives, on_device(): mine = lax.all_gather(tokens, 'tensor', axis=0, axis_index_groups=ring)  33.2 us
    ppermute x6, starting transfers between devices, other_core(): return lax.ppermute(value, 'tensor', swap)  31.4 us
    ppermute x12, waiting for transfers between devices, to_owner(): total = total + lax.ppermute(entry(ahead), 'dp', perm).astype(f32)  20.2 us
    unnamed x79, local copies, waits for them, and re-layouts  14.8 us
    pallas_call x1, Pallas kernels, on_device(): local_call(scan_kernel, (((rows, channels), bf16), ((rows, channels), f32...  11 us
  transfers between devices with their start and end apart: 24, of which 10 were waited for; matrix products, arithmetic and copies ran while one was open for 3% of the time, Pallas kernels for 7%

profile of v2, /device:TPU:1, one launch (start us, length us, event | category | flops | bytes accessed | tf_op | source)
XLA Modules:
  0.0 286.2 jit_solution(8736569224691765867)
XLA Ops:
  9.6 7.7 %all-to-all-start = ((bf16[16,256,256]{2,1,0:T(8,128)(2,1)}), bf16[16,256,256]{2,1,0:T(8,128)(2,1)S(1)}, u32[]{:S(2)}, u32[]{:S(2)}) async-start(bf16[16,256,256]{2,1,0:T(8,128)(2,1)} %broadcast_in_dim.16), calls=%async_computation | async-start | bytes 4194304 | tf_op jit(solution)/shard_map/all_to_all | solution.py:326
  18.1 33.2 %all-gather = bf16[2048,128]{1,0:T(8,128)(2,1)S(1)} all-gather(bf16[128,128]{1,0:T(8,128)(2,1)S(1)} %copy-done.36), channel_id=2, replica_groups={{0,2,4,6,8,10,12,14,16,18,20,22,24,26,28,30},{1,3,5,7,9,11,13,15,17,19,..., dimensions={0}, use_global_device_ids=true | all-gather | bytes 557056 | tf_op jit(solution)/shard_map/all_gather | solution.py:376
  51.3 8.0 %collective-permute-start = (bf16[16,128,128]{2,1,0:T(8,128)(2,1)S(1)}, bf16[16,128,128]{2,1,0:T(8,128)(2,1)S(1)}, u32[]{:S(2)}, u32[]{:S(2)}) collective-permute-start(bf16[16,128,128]{2,1,0:T(8,128)(2,1)S(1)} %bitcast.52), channel_id=1, source_target_pairs={{0,1},{1,0},{2,3},{3,2},{4,5},{5,4},{6,7},{7,6},{8,9},{9,8},{10,11... | collective-permute-start | bytes 1572872 | tf_op jit(solution)/shard_map/ppermute | solution.py:334
  66.6 41.0 %all_to_all.30.parts_ref = bf16[16,176,128]{2,1,0:T(8,128)(2,1)S(1)} all-to-all(bf16[16,176,128]{2,1,0:T(8,128)(2,1)S(1)} %shard_map.173), channel_id=1, replica_groups={{0,2,4,6,8,10,12,14,16,18,20,22,24,26,28,30},{1,3,5,7,9,11,13,15,17,19,..., dimensions={0} | all-to-all | bytes 1441792 | tf_op jit(solution)/shard_map/all_to_all | solution.py:326
  107.7 6.5 %collective-permute-start.2 = (bf16[16,128,128]{2,1,0:T(8,128)(2,1)S(1)}, bf16[16,128,128]{2,1,0:T(8,128)(2,1)}, u32[]{:S(2)}, u32[]{:S(2)}) collective-permute-start(bf16[16,128,128]{2,1,0:T(8,128)(2,1)S(1)} %slice.12.mine_ref), channel_id=1, source_target_pairs={{0,1},{1,0},{2,3},{3,2},{4,5},{5,4},{6,7},{7,6},{8,9},{9,8},{10,11... | collective-permute-start | bytes 1572872 | tf_op jit(solution)/shard_map/ppermute | solution.py:334
  116.5 5.4 %all-to-all-start.2 = ((bf16[16,8,544]{2,1,0:T(8,128)(2,1)}), bf16[16,8,544]{2,1,0:T(8,128)(2,1)S(1)}, u32[]{:S(2)}, u32[]{:S(2)}) async-start(bf16[16,8,544]{2,1,0:T(8,128)(2,1)} %shard_map.174), calls=%async_computation.2 | async-start | bytes 327680 | tf_op jit(solution)/shard_map/all_to_all | solution.py:326
  125.9 8.8 %all-to-all-done.2 = bf16[16,8,544]{2,1,0:T(8,128)(2,1)S(1)} async-done(((bf16[16,8,544]{2,1,0:T(8,128)(2,1)}), bf16[16,8,544]{2,1,0:T(8,128)(2,1)S(1)}, u32[]{:S(2)}, u32[]{:S(2)}) %all-to-all-start.2) | async-done | bytes 139296 | tf_op jit(solution)/shard_map/all_to_all | solution.py:326
  137.6 11.0 %shard_map.176 = (bf16[128,256]{1,0:T(8,128)(2,1)S(1)}, f32[128,256]{1,0:T(8,128)S(1)}, bf16[128,544]{1,0:T(8,128)(2,1)S(1)}) custom-call(bf16[128,544]{1,0:T(8,128)(2,1)S(1)} %bitcast.55, bf16[512,256]{1,0:T(8,128)(2,1)S(1)} %copy-done.21, f32[1,256]{1,0:T(1,128)S(1)} %bitcast.56, f32[16,256]{1,0:T(8,128)S(1)} %negate_bitcast_fusion.a_neg_ref, ...), custom_call_target="tpu_custom_call" | custom-call | tf_op jit(solution)/shard_map/pallas_call | solution.py:404
  149.2 4.0 %collective-permute-start.3 = (bf16[128,544]{1,0:T(8,128)(2,1)S(1)}, bf16[128,544]{1,0:T(8,128)(2,1)S(1)}, u32[]{:S(2)}, u32[]{:S(2)}) collective-permute-start(bf16[128,544]{1,0:T(8,128)(2,1)S(1)} %get-tuple-element.24.keep_ref), channel_id=1, source_target_pairs={{0,1},{1,0},{2,3},{3,2},{4,5},{5,4},{6,7},{7,6},{8,9},{9,8},{10,11... | collective-permute-start | bytes 417800 | tf_op jit(solution)/shard_map/ppermute | solution.py:334
  154.9 5.6 %all-to-all-start.3 = ((bf16[16,8,544]{2,1,0:T(8,128)(2,1)}), bf16[16,8,544]{2,1,0:T(8,128)(2,1)S(1)}, u32[]{:S(2)}, u32[]{:S(2)}) async-start(bf16[16,8,544]{2,1,0:T(8,128)(2,1)} %bitcast.7), calls=%async_computation.3 | async-start | bytes 327680 | tf_op jit(solution)/shard_map/all_to_all | solution.py:326
  161.4 3.3 %shard_map.178.refs_0_ = bf16[16,256,256]{2,1,0:T(8,128)(2,1)S(1)} custom-call(bf16[128,256]{1,0:T(8,128)(2,1)S(1)} %copy-done.19, bf16[16,128,256]{2,1,0:T(8,128)(2,1)S(1)} %copy-done.13, bf16[128,544]{1,0:T(8,128)(2,1)} %shard_map.177.after_ref), custom_call_target="tpu_custom_call" | custom-call | tf_op jit(solution)/shard_map/pallas_call | solution.py:411
  167.4 4.8 %collective-permute-start.7 = (bf16[4,256,256]{2,1,0:T(8,128)(2,1)}, bf16[4,256,256]{2,1,0:T(8,128)(2,1)}, u32[]{:S(2)}, u32[]{:S(2)}) collective-permute-start(bf16[4,256,256]{2,1,0:T(8,128)(2,1)} %get-tuple-element.42), channel_id=1, source_target_pairs={{0,384},{32,416},{64,448},{96,480},{128,0},{160,32},{192,64},{224,... | collective-permute-start | bytes 1572872 | tf_op jit(solution)/shard_map/ppermute | solution.py:365
  179.5 11.4 %all-to-all-start.4 = ((bf16[16,8,544]{2,1,0:T(8,128)(2,1)}), bf16[16,8,544]{2,1,0:T(8,128)(2,1)S(1)}, u32[]{:S(2)}, u32[]{:S(2)}) async-start(bf16[16,8,544]{2,1,0:T(8,128)(2,1)} %shard_map.179.after_ref), calls=%async_computation.4 | async-start | bytes 327680 | tf_op jit(solution)/shard_map/all_to_all | solution.py:326
  191.0 3.5 %shard_map.180 = (f32[16,128,128]{2,1,0:T(8,128)S(1)}, bf16[16,128,128]{2,1,0:T(8,128)(2,1)}) custom-call(bf16[128,256]{1,0:T(8,128)(2,1)S(1)} %copy-done.20, bf16[16,256,256]{2,1,0:T(8,128)(2,1)S(1)} %bitcast.49, s32[1,1]{1,0:T(1,128)} %bitcast.1.even_ref, bf16[16,8,544]{2,1,0:T(8,128)(2,1)} %shard_map.179.after_ref), custom_call_target="tpu_custom_call" | custom-call | tf_op jit(solution)/shard_map/pallas_call | solution.py:416
  195.5 4.1 %collective-permute-start.4 = (bf16[16,128,128]{2,1,0:T(8,128)(2,1)}, bf16[16,128,128]{2,1,0:T(8,128)(2,1)}, u32[]{:S(2)}, u32[]{:S(2)}) collective-permute-start(bf16[16,128,128]{2,1,0:T(8,128)(2,1)} %get-tuple-element.27), channel_id=1, source_target_pairs={{0,1},{1,0},{2,3},{3,2},{4,5},{5,4},{6,7},{7,6},{8,9},{9,8},{10,11... | collective-permute-start | bytes 1572872 | tf_op jit(solution)/shard_map/ppermute | solution.py:334
  204.3 3.3 %shard_map.181 = (bf16[128,256]{1,0:T(8,128)(2,1)S(1)}, f32[16,128,128]{2,1,0:T(8,128)S(1)}, bf16[16,128,128]{2,1,0:T(8,128)(2,1)S(1)}) custom-call(bf16[128,544]{1,0:T(8,128)(2,1)S(1)} %bitcast.54, bf16[256,512]{1,0:T(8,128)(2,1)S(1)} %copy-done.15, bf16[256,32]{1,0:T(8,128)(2,1)S(1)} %copy-done.17, f32[128,256]{1,0:T(8,128)S(1)} %copy-done.25, ...), custom_call_target="tpu_custom_call" | custom-call | tf_op jit(solution)/shard_map/pallas_call | solution.py:422
  207.7 6.6 %collective-permute-start.8 = (bf16[16,128,128]{2,1,0:T(8,128)(2,1)S(1)}, bf16[16,128,128]{2,1,0:T(8,128)(2,1)S(1)}, u32[]{:S(2)}, u32[]{:S(2)}) collective-permute-start(bf16[16,128,128]{2,1,0:T(8,128)(2,1)S(1)} %get-tuple-element.31), channel_id=1, source_target_pairs={{0,1},{1,0},{2,3},{3,2},{4,5},{5,4},{6,7},{7,6},{8,9},{9,8},{10,11... | collective-permute-start | bytes 1572872 | tf_op jit(solution)/shard_map/ppermute | solution.py:334
  214.2 3.4 %shard_map.182.after_ref = bf16[4,4,256,256]{3,2,1,0:T(8,128)(2,1)S(1)} custom-call(bf16[128,256]{1,0:T(8,128)(2,1)S(1)} %get-tuple-element.32.d_inner_ref, bf16[16,128,256]{2,1,0:T(8,128)(2,1)S(1)} %copy-done.11), custom_call_target="tpu_custom_call" | custom-call | tf_op jit(solution)/shard_map/pallas_call | solution.py:431
  219.9 7.1 %all-to-all-start.5 = ((bf16[16,256,128]{2,1,0:T(8,128)(2,1)}), bf16[16,256,128]{2,1,0:T(8,128)(2,1)}, u32[]{:S(2)}, u32[]{:S(2)}) async-start(bf16[16,256,128]{2,1,0:T(8,128)(2,1)} %copy-done.6), calls=%async_computation.5 | async-start | bytes 2097152 | tf_op jit(solution)/shard_map/all_to_all | solution.py:326
  235.7 4.4 %collective-permute-start.17 = (bf16[256,256]{1,0:T(8,128)(2,1)S(1)}, bf16[256,256]{1,0:T(8,128)(2,1)S(1)}, u32[]{:S(2)}, u32[]{:S(2)}) collective-permute-start(bf16[256,256]{1,0:T(8,128)(2,1)S(1)} %get-tuple-element.45), channel_id=1, source_target_pairs={{0,96},{32,0},{64,32},{96,64},{128,224},{160,128},{192,160},{224,1... | collective-permute-start | bytes 393224 | tf_op jit(solution)/shard_map/ppermute | solution.py:365
  243.5 3.2 %collective-permute-start.15 = (bf16[256,256]{1,0:T(8,128)(2,1)S(1)}, bf16[256,256]{1,0:T(8,128)(2,1)S(1)}, u32[]{:S(2)}, u32[]{:S(2)}) collective-permute-start(bf16[256,256]{1,0:T(8,128)(2,1)S(1)} %get-tuple-element.44), channel_id=1, source_target_pairs={{0,32},{32,64},{64,96},{96,0},{128,160},{160,192},{192,224},{224,1... | collective-permute-start | bytes 393224 | tf_op jit(solution)/shard_map/ppermute | solution.py:365
  246.8 12.7 %collective-permute-done.9 = bf16[4,256,256]{2,1,0:T(8,128)(2,1)} collective-permute-done((bf16[4,256,256]{2,1,0:T(8,128)(2,1)S(1)}, bf16[4,256,256]{2,1,0:T(8,128)(2,1)}, u32[]{:S(2)}, u32[]{:S(2)}) %collective-permute-start.9) | collective-permute-done | bytes 524320 | tf_op jit(solution)/shard_map/ppermute | solution.py:365
  261.1 4.2 %collective-permute-start.14 = (bf16[256,256]{1,0:T(8,128)(2,1)S(1)}, bf16[256,256]{1,0:T(8,128)(2,1)S(1)}, u32[]{:S(2)}, u32[]{:S(2)}) collective-permute-start(bf16[256,256]{1,0:T(8,128)(2,1)S(1)} %get-tuple-element.48), channel_id=1, source_target_pairs={{0,96},{32,0},{64,32},{96,64},{128,224},{160,128},{192,160},{224,1... | collective-permute-start | bytes 393224 | tf_op jit(solution)/shard_map/ppermute | solution.py:365
  273.0 3.4 %collective-permute-done.12 = bf16[256,256]{1,0:T(8,128)(2,1)S(1)} collective-permute-done((bf16[256,256]{1,0:T(8,128)(2,1)S(1)}, bf16[256,256]{1,0:T(8,128)(2,1)S(1)}, u32[]{:S(2)}, u32[]{:S(2)}) %collective-permute-start.12) | collective-permute-done | bytes 131104 | tf_op jit(solution)/shard_map/ppermute | solution.py:365
  (131 shorter events, 64.9 us)
Async XLA Ops:
  9.6 51.2 %all-to-all-start = ((bf16[16,256,256]{2,1,0:T(8,128)(2,1)}), bf16[16,256,256]{2,1,0:T(8,128)(2,1)S(1)}, u32[]{:S(2)}, u32[]{:S(2)}) async-start(bf16[16,256,256]{2,1,0:T(8,128)(2,1)} %broadcast_in_dim.16), calls=%async_computation | async-start | bytes 4194304 | tf_op jit(solution)/shard_map/all_to_all | solution.py:326
  17.3 96.8 %all-gather.4.cloned.1.call-start = ((), (), s32[]{:S(2)}) async-start(), calls=%async_computation.6 | async-start | bytes 2228224 | tf_op jit(solution)/shard_map/all_gather | solution.py:375
  51.3 9.5 %collective-permute-start = (bf16[16,128,128]{2,1,0:T(8,128)(2,1)S(1)}, bf16[16,128,128]{2,1,0:T(8,128)(2,1)S(1)}, u32[]{:S(2)}, u32[]{:S(2)}) collective-permute-start(bf16[16,128,128]{2,1,0:T(8,128)(2,1)S(1)} %bitcast.52), channel_id=1, source_target_pairs={{0,1},{1,0},{2,3},{3,2},{4,5},{5,4},{6,7},{7,6},{8,9},{9,8},{10,11... | collective-permute-start | bytes 1572872 | tf_op jit(solution)/shard_map/ppermute | solution.py:334
  63.2 3.3 %collective-permute-start.1 = (bf16[128,544]{1,0:T(8,128)(2,1)S(1)}, bf16[128,544]{1,0:T(8,128)(2,1)S(1)}, u32[]{:S(2)}, u32[]{:S(2)}) collective-permute-start(bf16[128,544]{1,0:T(8,128)(2,1)S(1)} %get-tuple-element.20.mine_ref), channel_id=1, source_target_pairs={{0,1},{1,0},{2,3},{3,2},{4,5},{5,4},{6,7},{7,6},{8,9},{9,8},{10,11... | collective-permute-start | bytes 417800 | tf_op jit(solution)/shard_map/ppermute | solution.py:334
  107.7 14.2 %collective-permute-start.2 = (bf16[16,128,128]{2,1,0:T(8,128)(2,1)S(1)}, bf16[16,128,128]{2,1,0:T(8,128)(2,1)}, u32[]{:S(2)}, u32[]{:S(2)}) collective-permute-start(bf16[16,128,128]{2,1,0:T(8,128)(2,1)S(1)} %slice.12.mine_ref), channel_id=1, source_target_pairs={{0,1},{1,0},{2,3},{3,2},{4,5},{5,4},{6,7},{7,6},{8,9},{9,8},{10,11... | collective-permute-start | bytes 1572872 | tf_op jit(solution)/shard_map/ppermute | solution.py:334
  116.5 18.3 %all-to-all-start.2 = ((bf16[16,8,544]{2,1,0:T(8,128)(2,1)}), bf16[16,8,544]{2,1,0:T(8,128)(2,1)S(1)}, u32[]{:S(2)}, u32[]{:S(2)}) async-start(bf16[16,8,544]{2,1,0:T(8,128)(2,1)} %shard_map.174), calls=%async_computation.2 | async-start | bytes 327680 | tf_op jit(solution)/shard_map/all_to_all | solution.py:326
  149.2 5.0 %collective-permute-start.3 = (bf16[128,544]{1,0:T(8,128)(2,1)S(1)}, bf16[128,544]{1,0:T(8,128)(2,1)S(1)}, u32[]{:S(2)}, u32[]{:S(2)}) collective-permute-start(bf16[128,544]{1,0:T(8,128)(2,1)S(1)} %get-tuple-element.24.keep_ref), channel_id=1, source_target_pairs={{0,1},{1,0},{2,3},{3,2},{4,5},{5,4},{6,7},{7,6},{8,9},{9,8},{10,11... | collective-permute-start | bytes 417800 | tf_op jit(solution)/shard_map/ppermute | solution.py:334
  154.9 22.3 %all-to-all-start.3 = ((bf16[16,8,544]{2,1,0:T(8,128)(2,1)}), bf16[16,8,544]{2,1,0:T(8,128)(2,1)S(1)}, u32[]{:S(2)}, u32[]{:S(2)}) async-start(bf16[16,8,544]{2,1,0:T(8,128)(2,1)} %bitcast.7), calls=%async_computation.3 | async-start | bytes 327680 | tf_op jit(solution)/shard_map/all_to_all | solution.py:326
  167.4 32.2 %collective-permute-start.7 = (bf16[4,256,256]{2,1,0:T(8,128)(2,1)}, bf16[4,256,256]{2,1,0:T(8,128)(2,1)}, u32[]{:S(2)}, u32[]{:S(2)}) collective-permute-start(bf16[4,256,256]{2,1,0:T(8,128)(2,1)} %get-tuple-element.42), channel_id=1, source_target_pairs={{0,384},{32,416},{64,448},{96,480},{128,0},{160,32},{192,64},{224,... | collective-permute-start | bytes 1572872 | tf_op jit(solution)/shard_map/ppermute | solution.py:365
  172.2 27.4 %collective-permute-start.6 = (bf16[4,256,256]{2,1,0:T(8,128)(2,1)}, bf16[4,256,256]{2,1,0:T(8,128)(2,1)}, u32[]{:S(2)}, u32[]{:S(2)}) collective-permute-start(bf16[4,256,256]{2,1,0:T(8,128)(2,1)} %get-tuple-element.43), channel_id=1, source_target_pairs={{0,256},{32,288},{64,320},{96,352},{128,384},{160,416},{192,448},{... | collective-permute-start | bytes 1572872 | tf_op jit(solution)/shard_map/ppermute | solution.py:365
  174.8 26.2 %collective-permute-start.5 = (bf16[4,256,256]{2,1,0:T(8,128)(2,1)}, bf16[4,256,256]{2,1,0:T(8,128)(2,1)}, u32[]{:S(2)}, u32[]{:S(2)}) collective-permute-start(bf16[4,256,256]{2,1,0:T(8,128)(2,1)} %get-tuple-element.41), channel_id=1, source_target_pairs={{0,128},{32,160},{64,192},{96,224},{128,256},{160,288},{192,320},{... | collective-permute-start | bytes 1572872 | tf_op jit(solution)/shard_map/ppermute | solution.py:365
  179.5 23.6 %all-to-all-start.4 = ((bf16[16,8,544]{2,1,0:T(8,128)(2,1)}), bf16[16,8,544]{2,1,0:T(8,128)(2,1)S(1)}, u32[]{:S(2)}, u32[]{:S(2)}) async-start(bf16[16,8,544]{2,1,0:T(8,128)(2,1)} %shard_map.179.after_ref), calls=%async_computation.4 | async-start | bytes 327680 | tf_op jit(solution)/shard_map/all_to_all | solution.py:326
  195.5 22.1 %collective-permute-start.4 = (bf16[16,128,128]{2,1,0:T(8,128)(2,1)}, bf16[16,128,128]{2,1,0:T(8,128)(2,1)}, u32[]{:S(2)}, u32[]{:S(2)}) collective-permute-start(bf16[16,128,128]{2,1,0:T(8,128)(2,1)} %get-tuple-element.27), channel_id=1, source_target_pairs={{0,1},{1,0},{2,3},{3,2},{4,5},{5,4},{6,7},{7,6},{8,9},{9,8},{10,11... | collective-permute-start | bytes 1572872 | tf_op jit(solution)/shard_map/ppermute | solution.py:334
  207.7 10.0 %collective-permute-start.8 = (bf16[16,128,128]{2,1,0:T(8,128)(2,1)S(1)}, bf16[16,128,128]{2,1,0:T(8,128)(2,1)S(1)}, u32[]{:S(2)}, u32[]{:S(2)}) collective-permute-start(bf16[16,128,128]{2,1,0:T(8,128)(2,1)S(1)} %get-tuple-element.31), channel_id=1, source_target_pairs={{0,1},{1,0},{2,3},{3,2},{4,5},{5,4},{6,7},{7,6},{8,9},{9,8},{10,11... | collective-permute-start | bytes 1572872 | tf_op jit(solution)/shard_map/ppermute | solution.py:334
  219.9 57.5 %all-to-all-start.5 = ((bf16[16,256,128]{2,1,0:T(8,128)(2,1)}), bf16[16,256,128]{2,1,0:T(8,128)(2,1)}, u32[]{:S(2)}, u32[]{:S(2)}) async-start(bf16[16,256,128]{2,1,0:T(8,128)(2,1)} %copy-done.6), calls=%async_computation.5 | async-start | bytes 2097152 | tf_op jit(solution)/shard_map/all_to_all | solution.py:326
  228.1 15.4 %collective-permute-start.11 = (bf16[4,256,256]{2,1,0:T(8,128)(2,1)}, bf16[4,256,256]{2,1,0:T(8,128)(2,1)}, u32[]{:S(2)}, u32[]{:S(2)}) collective-permute-start(bf16[4,256,256]{2,1,0:T(8,128)(2,1)} %get-tuple-element.39), channel_id=1, source_target_pairs={{0,384},{32,416},{64,448},{96,480},{128,0},{160,32},{192,64},{224,... | collective-permute-start | bytes 1572872 | tf_op jit(solution)/shard_map/ppermute | solution.py:365
  230.6 16.1 %collective-permute-start.10 = (bf16[4,256,256]{2,1,0:T(8,128)(2,1)}, bf16[4,256,256]{2,1,0:T(8,128)(2,1)}, u32[]{:S(2)}, u32[]{:S(2)}) collective-permute-start(bf16[4,256,256]{2,1,0:T(8,128)(2,1)} %get-tuple-element.40), channel_id=1, source_target_pairs={{0,256},{32,288},{64,320},{96,352},{128,384},{160,416},{192,448},{... | collective-permute-start | bytes 1572872 | tf_op jit(solution)/shard_map/ppermute | solution.py:365
  233.7 25.8 %collective-permute-start.9 = (bf16[4,256,256]{2,1,0:T(8,128)(2,1)S(1)}, bf16[4,256,256]{2,1,0:T(8,128)(2,1)}, u32[]{:S(2)}, u32[]{:S(2)}) collective-permute-start(bf16[4,256,256]{2,1,0:T(8,128)(2,1)S(1)} %get-tuple-element.38), channel_id=1, source_target_pairs={{0,128},{32,160},{64,192},{96,224},{128,256},{160,288},{192,320},{... | collective-permute-start | bytes 1572872 | tf_op jit(solution)/shard_map/ppermute | solution.py:365
  235.7 32.0 %collective-permute-start.17 = (bf16[256,256]{1,0:T(8,128)(2,1)S(1)}, bf16[256,256]{1,0:T(8,128)(2,1)S(1)}, u32[]{:S(2)}, u32[]{:S(2)}) collective-permute-start(bf16[256,256]{1,0:T(8,128)(2,1)S(1)} %get-tuple-element.45), channel_id=1, source_target_pairs={{0,96},{32,0},{64,32},{96,64},{128,224},{160,128},{192,160},{224,1... | collective-permute-start | bytes 393224 | tf_op jit(solution)/shard_map/ppermute | solution.py:365
  240.1 30.1 %collective-permute-start.16 = (bf16[256,256]{1,0:T(8,128)(2,1)S(1)}, bf16[256,256]{1,0:T(8,128)(2,1)S(1)}, u32[]{:S(2)}, u32[]{:S(2)}) collective-permute-start(bf16[256,256]{1,0:T(8,128)(2,1)S(1)} %get-tuple-element.46), channel_id=1, source_target_pairs={{0,64},{32,96},{64,0},{96,32},{128,192},{160,224},{192,128},{224,1... | collective-permute-start | bytes 393224 | tf_op jit(solution)/shard_map/ppermute | solution.py:365
  243.5 26.7 %collective-permute-start.15 = (bf16[256,256]{1,0:T(8,128)(2,1)S(1)}, bf16[256,256]{1,0:T(8,128)(2,1)S(1)}, u32[]{:S(2)}, u32[]{:S(2)}) collective-permute-start(bf16[256,256]{1,0:T(8,128)(2,1)S(1)} %get-tuple-element.44), channel_id=1, source_target_pairs={{0,32},{32,64},{64,96},{96,0},{128,160},{160,192},{192,224},{224,1... | collective-permute-start | bytes 393224 | tf_op jit(solution)/shard_map/ppermute | solution.py:365
  261.1 10.1 %collective-permute-start.14 = (bf16[256,256]{1,0:T(8,128)(2,1)S(1)}, bf16[256,256]{1,0:T(8,128)(2,1)S(1)}, u32[]{:S(2)}, u32[]{:S(2)}) collective-permute-start(bf16[256,256]{1,0:T(8,128)(2,1)S(1)} %get-tuple-element.48), channel_id=1, source_target_pairs={{0,96},{32,0},{64,32},{96,64},{128,224},{160,128},{192,160},{224,1... | collective-permute-start | bytes 393224 | tf_op jit(solution)/shard_map/ppermute | solution.py:365
  265.3 7.8 %collective-permute-start.13 = (bf16[256,256]{1,0:T(8,128)(2,1)S(1)}, bf16[256,256]{1,0:T(8,128)(2,1)S(1)}, u32[]{:S(2)}, u32[]{:S(2)}) collective-permute-start(bf16[256,256]{1,0:T(8,128)(2,1)S(1)} %get-tuple-element.49), channel_id=1, source_target_pairs={{0,64},{32,96},{64,0},{96,32},{128,192},{160,224},{192,128},{224,1... | collective-permute-start | bytes 393224 | tf_op jit(solution)/shard_map/ppermute | solution.py:365
  267.8 8.7 %collective-permute-start.12 = (bf16[256,256]{1,0:T(8,128)(2,1)S(1)}, bf16[256,256]{1,0:T(8,128)(2,1)S(1)}, u32[]{:S(2)}, u32[]{:S(2)}) collective-permute-start(bf16[256,256]{1,0:T(8,128)(2,1)S(1)} %get-tuple-element.47), channel_id=1, source_target_pairs={{0,32},{32,64},{64,96},{96,0},{128,160},{160,192},{192,224},{224,1... | collective-permute-start | bytes 393224 | tf_op jit(solution)/shard_map/ppermute | solution.py:365
  (39 other events, 583.9 us)
Sparse Core Ops, SparseCore 0:
  21.2 65.4 all-gather.3
